TPU v7x, 256 devices: a whole 4x4x8 slice. The times are simulated.
256 devices in a mesh: dp: 16 (over z_hi, x), fsdp: 16 (over y, z_lo, core).
Axes of the slice: x: 4, y: 4, z: 8 (z_hi: 4, z_lo: 2; z = z_hi * 2 + z_lo), core: 2. Of those that a mesh axis runs over, the one named last changes fastest.
Arguments:
- hidden: bfloat16 [12288, 14336], P('fsdp', 'dp'), may hold values from -6 to 6
- cotangent: bfloat16 [12288, 4096], P('fsdp'), may hold values from -6 to 6
- weight: bfloat16 [14336, 4096], P('dp', 'fsdp'), may hold values from -0.0625 to 0.0625
- basis: bfloat16 [14336, 512], P('dp'), may hold values from -0.0625 to 0.0625
- first_moment: float32 [512, 4096], P('dp', 'fsdp'), may hold values from -665.1075 to 665.1075
- second_moment: float32 [512, 4096], P('dp', 'fsdp'), may hold values from 13 to 3076
Outputs:
- output: bfloat16 [12288, 4096], P('fsdp', 'dp')
- act_grad: bfloat16 [12288, 14336], P('fsdp', 'dp')
- new_first: float32 [512, 4096], P('dp', 'fsdp')
- new_second: float32 [512, 4096], P('dp', 'fsdp')
- update: bfloat16 [14336, 4096], P('dp', 'fsdp')
All inputs are finite; a program needn't handle non-finite values.
Results may differ from a plain program's by a relative error of at most 0.0051.
Values may be sent and summed in bfloat16 or wider, within the bound.
No kernel may reach another device: no remote copies, remote signals or barrier semaphores. Data moves between devices by JAX's collectives and lax.ppermute only.
A program may use at most 128 MiB of HBM per device.

v0:
```python
import jax
import jax.numpy as jnp
from jax import lax
from jax.sharding import PartitionSpec as P

STEP = 20


def on_device(hidden, cotangent, weight, basis, first_moment, second_moment):
    act_grad = lax.dot_general(
        cotangent,
        lax.all_gather(weight, "fsdp", axis=1, tiled=True),
        (((1,), (1,)), ((), ())),
        preferred_element_type=jnp.float32,
    )
    partial_out = jnp.dot(
        hidden,
        lax.all_gather(weight, "fsdp", axis=1, tiled=True),
        preferred_element_type=jnp.float32,
    )
    output = lax.psum_scatter(partial_out, "dp", scatter_dimension=1, tiled=True).astype(
        jnp.bfloat16
    )
    low_part = jnp.dot(hidden, basis, preferred_element_type=jnp.float32)
    rank_here = first_moment.shape[0]
    low_whole = lax.psum(low_part, "dp").astype(jnp.bfloat16)
    low_mine = lax.dynamic_slice_in_dim(low_whole, lax.axis_index("dp") * rank_here, rank_here, 1)
    grad_part = lax.dot_general(
        low_mine, cotangent, (((0,), (0,)), ((), ())), preferred_element_type=jnp.float32
    )
    grad = lax.psum_scatter(grad_part, "fsdp", scatter_dimension=1, tiled=True)
    new_first = 0.9 * first_moment + 0.1 * grad
    new_second = 0.999 * second_moment + 0.001 * grad * grad
    first_fix = 1.0 - 0.9**STEP
    second_fix = 1.0 - 0.999**STEP
    normed = (new_first / first_fix / (jnp.sqrt(new_second / second_fix) + 1e-08)).astype(
        jnp.bfloat16
    )
    normed_all = lax.all_gather(normed, "dp", axis=0, tiled=True)
    update = jnp.dot(basis, normed_all, preferred_element_type=jnp.float32).astype(jnp.bfloat16)
    return (output, act_grad.astype(jnp.bfloat16), new_first, new_second, update)


def solution(mesh):
    in_specs = (
        P("fsdp", "dp"),
        P("fsdp", None),
        P("dp", "fsdp"),
        P("dp", None),
        P("dp", "fsdp"),
        P("dp", "fsdp"),
    )
    out_specs = (
        P("fsdp", "dp"),
        P("fsdp", "dp"),
        P("dp", "fsdp"),
        P("dp", "fsdp"),
        P("dp", "fsdp"),
    )
    return jax.shard_map(
        on_device, mesh=mesh, in_specs=in_specs, out_specs=out_specs, check_vma=False
    )
```

profile of v0, /device:TPU:32, one launch (start us, length us, event | category | flops | bytes accessed | tf_op | source)
XLA Modules:
  0.0 366.1 jit_solution(7738518977697509446)
XLA Ops:
  7.2 0.0 copy-start
  7.2 0.0 all-gather.2.cloned.1.call-start
  7.2 0.7 all-gather.2.cloned.1.call-update
  7.9 0.0 reduce-scatter.5.cloned.1.call-start
  8.0 0.5 copy-done
  8.5 2.1 fusion.6
  10.7 117.5 %all-reduce.1 = bf16[768,512]{1,0:T(8,128)(2,1)} all-reduce(f32[768,512]{1,0:T(8,128)S(1)} %fusion.6), channel_id=1, replica_groups=mesh['dp'=16,'fsdp'=16] {'dp'}, use_global_device_ids=true, to_apply=%region_1.0 | all-reduce | flops 393216 | bytes 2359296 | tf_op jit(solution)/shard_map/psum | solution.py:26
  128.1 5.0 %fusion.1 = f32[32,4096]{1,0:T(8,128)} fusion(bf16[768,4096]{1,0:T(8,128)(2,1)} %param.7, bf16[768,512]{1,0:T(8,128)(2,1)} %all-reduce.1, s32[]{:T(128)S(6)} %select_n.3), kind=kOutput, calls=%fused_computation.4 | convolution fusion | flops 201326592 | bytes 7012356 | tf_op jit(solution)/shard_map/dot_general | solution.py:28
  133.1 0.0 reduce-scatter.5.cloned.1.call-update
  133.1 0.0 reduce-scatter.3.cloned.1.call-start
  133.2 0.0 all-gather.2.cloned.1.call-done
  133.2 12.1 %fusion.5 = f32[768,4096]{1,0:T(8,128)} fusion(bf16[768,896]{1,0:T(8,128)(2,1)S(1)} %copy-done, bf16[896,4096]{1,0:T(8,128)(2,1)} %all-gather.2.cloned.1.call-done), kind=kOutput, calls=%fused_computation.10 | convolution fusion | flops 5637144576 | bytes 21299200 | tf_op jit(solution)/shard_map/dot_general | solution.py:16
  145.3 0.0 copy-start.2
  145.3 0.0 copy-start.3
  145.3 0.0 copy-start.1
  145.3 0.0 reduce-scatter.3.cloned.1.call-update
  145.3 47.6 %reduce-scatter.5.cloned.1.call-done = f32[32,256]{1,0:T(8,128)} async-done(((f32[32,4096]{1,0:T(8,128)}), f32[32,256]{1,0:T(8,128)}) %reduce-scatter.5.cloned.1.call-update) | async-done | bytes 32784 | tf_op jit(solution)/shard_map/reduce_scatter | solution.py:31
  192.9 0.0 copy-done.2
  192.9 0.0 copy-done.3
  192.9 1.4 divide_convert_fusion
  194.3 51.9 %all_gather.8 = bf16[512,256]{1,0:T(8,128)(2,1)S(1)} all-gather(bf16[32,256]{1,0:T(8,128)(2,1)S(1)} %get-tuple-element.10), channel_id=1, replica_groups=mesh['dp'=16,'fsdp'=16] {'dp'}, dimensions={0}, use_global_device_ids=true | all-gather | bytes 278528 | tf_op jit(solution)/shard_map/all_gather | solution.py:39
  246.2 0.0 copy-done.1
  246.2 0.5 fusion
  246.7 1.0 copy.11
  247.7 11.9 %convolution_convert_fusion = bf16[768,896]{1,0:T(8,128)(2,1)} fusion(bf16[768,4096]{1,0:T(8,128)(2,1)} %param.7, bf16[896,4096]{1,0:T(8,128)(2,1)} %all-gather.2.cloned.1.call-done), kind=kOutput, calls=%fused_computation | convolution fusion | flops 5637832704 | bytes 15007744 | tf_op jit(solution)/shard_map/dot_general | solution.py:10
  259.6 98.1 %reduce-scatter.3.cloned.1.call-done = f32[768,256]{1,0:T(8,128)} async-done(((f32[768,4096]{1,0:T(8,128)}), f32[768,256]{1,0:T(8,128)}) %reduce-scatter.3.cloned.1.call-update) | async-done | bytes 786448 | tf_op jit(solution)/shard_map/reduce_scatter | solution.py:21
  357.7 1.9 convert_element_type.18
Async XLA Ops:
  7.2 1.3 copy-start
  7.2 126.0 %all-gather.2.cloned.1.call-start = ((), (), s32[]{:S(2)}) async-start(), calls=%async_computation.2 | async-start | bytes 7798784 | tf_op jit(solution)/shard_map/all_gather | solution.py:18
  7.9 185.0 %reduce-scatter.5.cloned.1.call-start = ((), (), s32[]{:S(2)}) async-start(), calls=%async_computation.4 | async-start | bytes 557056 | tf_op jit(solution)/shard_map/reduce_scatter | solution.py:31
  133.1 224.5 %reduce-scatter.3.cloned.1.call-start = ((), (), s32[]{:S(2)}) async-start(), calls=%async_computation.3 | async-start | bytes 13369344 | tf_op jit(solution)/shard_map/reduce_scatter | solution.py:21
  145.3 47.6 %copy-start.2 = (f32[32,256]{1,0:T(8,128)S(1)}, f32[32,256]{1,0:T(8,128)}, u32[]{:S(2)}) copy-start(f32[32,256]{1,0:T(8,128)} %param.11) | copy-start | bytes 98308
  145.3 47.6 %copy-start.3 = (f32[32,256]{1,0:T(8,128)S(1)}, f32[32,256]{1,0:T(8,128)}, u32[]{:S(2)}) copy-start(f32[32,256]{1,0:T(8,128)} %param.10) | copy-start | bytes 98308
  145.3 100.9 %copy-start.1 = (bf16[896,512]{1,0:T(8,128)(2,1)S(1)}, bf16[896,512]{1,0:T(8,128)(2,1)}, u32[]{:S(2)}) copy-start(bf16[896,512]{1,0:T(8,128)(2,1)} %param.9) | copy-start | bytes 2752516
Sparse Core Ops, SparseCore 0:
  9.8 94.8 all-gather.1
  133.3 59.6 reduce-scatter.4
  197.1 160.4 reduce-scatter.2
where the time goes:
time: 371 us; the launch traced here: 366 us
  blocking collectives  169 us (46%)
  waiting for transfers between devices  146 us (39%)
  matrix products  31.6 us (9%)
  between operations  13.8 us (4%)
    psum x1, blocking collectives, on_device(): low_whole = lax.psum(low_part, 'dp').astype(jnp.bfloat16)  117 us
    reduce_scatter x1, waiting for transfers between devices, on_device(): lax.psum_scatter(partial_out, 'dp', scatter_dimension=1, tiled=True)  98.1 us
    all_gather x1, blocking collectives, on_device(): normed_all = lax.all_gather(normed, 'dp', axis=0, tiled=True)  51.9 us
    reduce_scatter x1, waiting for transfers between devices, on_device(): grad = lax.psum_scatter(grad_part, 'fsdp', scatter_dimension=1, tiled=True)  47.6 us
    dot_general x1, matrix products, on_device(): jnp.dot(hidden, lax.all_gather(weight, 'fsdp', axis=1, tiled=True), prefe...  12.1 us
    dot_general x1, matrix products, on_device(): lax.dot_general(cotangent, lax.all_gather(weight, 'fsdp', axis=1, tiled=T...  11.9 us
  transfers between devices with their start and end apart: 3, of which 2 were waited for; matrix products, arithmetic and copies ran while one was open for 9% of the time, Pallas kernels for 0%

commit v1 on v0

v1 whole, which is shorter than its diff:
```python
import functools

import jax
import jax.numpy as jnp
from jax import lax
from jax.experimental import pallas as pl
from jax.experimental.pallas import tpu as pltpu
from jax.sharding import Mesh
from jax.sharding import PartitionSpec as P

STEP = 20
BF = jnp.bfloat16
F32 = jnp.float32
AXES = ("zh", "x", "y", "zl", "c")
SIZE = dict(zh=4, x=4, y=4, zl=2, c=2)
FSDP = ("y", "zl", "c")
COLS = 128
MIB = 1024 * 1024


def shift(array, axis, by):
    n = SIZE[axis]
    return lax.ppermute(array, axis, [(i, (i + by) % n) for i in range(n)])


def partial_kernel(half, pick, h_ref, w0, w1, w2, w3, far_up, far_down, near_up, near_down, acc_up, acc_down, own, wide):
    k = pl.program_id(0)
    for block, w in enumerate((w0, w1, w2, w3)):
        wide[:, block * COLS : (block + 1) * COLS] = w[0]
    top = jnp.dot(h_ref[:half], wide[...], preferred_element_type=F32)
    low = jnp.dot(h_ref[half:], wide[...], preferred_element_type=F32)

    @pl.when(k == 0)
    def _():
        far_up[...] = top.astype(BF)
        far_down[...] = low.astype(BF)

    @pl.when(k == 1)
    def _():
        acc_up[...] = top
        near_up[...] = low.astype(BF)

    @pl.when(k == 2)
    def _():
        near_down[...] = top.astype(BF)
        acc_down[...] = low

    @pl.when(k == 3)
    def _():
        own[:half] = top
        own[half:] = low


def partials(hidden, shards, dests):
    tokens, full = hidden.shape
    half = tokens // 2
    width = 4 * COLS
    small = pltpu.HBM((half, width), BF)
    kept = pltpu.HBM((half, width), F32)
    whole = pltpu.HBM((tokens, width), F32)

    def same(k, s):
        return (0, 0)

    def weight_spec(block):
        return pl.BlockSpec((1, full, COLS), lambda k, s: (4 * block + s[k], 0, 0))

    return pl.pallas_call(
        functools.partial(partial_kernel, half),
        out_shape=[small] * 4 + [kept] * 2 + [whole],
        grid_spec=pltpu.PrefetchScalarGridSpec(
            num_scalar_prefetch=1,
            grid=(4,),
            in_specs=[pl.BlockSpec((tokens, full), same)] + [weight_spec(b) for b in range(4)],
            out_specs=[pl.BlockSpec((half, width), same)] * 6 + [pl.BlockSpec((tokens, width), same)],
            scratch_shapes=[pltpu.VMEM((full, width), BF)],
        ),
        compiler_params=pltpu.CompilerParams(vmem_limit_bytes=24 * MIB),
        cost_estimate=pl.CostEstimate(
            flops=8 * tokens * full * width, bytes_accessed=8 * MIB, transcendentals=0
        ),
        name="partials",
    )(dests, hidden, shards, shards, shards, shards)


def add_kernel(a, b, ra, rb, out_a, out_b):
    out_a[...] = (a[...] + ra[...].astype(F32)).astype(BF)
    out_b[...] = (b[...] + rb[...].astype(F32)).astype(BF)


def add_pair(a, b, ra, rb):
    rows, width = a.shape
    tile = rows // 3
    spec = pl.BlockSpec((tile, width), lambda i: (i, 0))
    return pl.pallas_call(
        add_kernel,
        out_shape=[pltpu.HBM(a.shape, BF)] * 2,
        grid=(3,),
        in_specs=[spec] * 4,
        out_specs=[spec] * 2,
        compiler_params=pltpu.CompilerParams(vmem_limit_bytes=8 * MIB),
        cost_estimate=pl.CostEstimate(flops=2 * a.size, bytes_accessed=16 * a.size, transcendentals=0),
        name="add_pair",
    )(a, b, ra, rb)


def regroup_kernel(pick, own, last_up, near_dn, near_up, last_dn, *outs):
    i = pl.program_id(0)
    mine = own[...]
    first = mine + last_up[...].astype(F32) + near_dn[...].astype(F32)
    second = mine + near_up[...].astype(F32) + last_dn[...].astype(F32)
    own_total = outs[4]
    own_total[...] = jnp.where(i == 0, first, second)
    for k in range(4):
        cols = pl.ds(pl.multiple_of(pick[k] * COLS, COLS), COLS)
        outs[k][...] = own_total[:, cols].astype(outs[k].dtype)


def regroup(own, got, pick):
    rows, width = own.shape
    half = rows // 2
    part = pl.BlockSpec((half, width), lambda i, s: (0, 0))
    return pl.pallas_call(
        regroup_kernel,
        out_shape=[pltpu.HBM((rows, COLS), BF)] * 3 + [pltpu.HBM((rows, COLS), F32)],
        grid_spec=pltpu.PrefetchScalarGridSpec(
            num_scalar_prefetch=1,
            grid=(2,),
            in_specs=[pl.BlockSpec((half, width), lambda i, s: (i, 0))] + [part] * 4,
            out_specs=[pl.BlockSpec((half, COLS), lambda i, s: (i, 0))] * 4,
            scratch_shapes=[pltpu.VMEM((half, width), F32)],
        ),
        compiler_params=pltpu.CompilerParams(vmem_limit_bytes=12 * MIB),
        cost_estimate=pl.CostEstimate(flops=rows * 4096, bytes_accessed=4 * MIB, transcendentals=0),
        name="regroup",
    )(pick, own, *got)


def finish_kernel(*refs):
    out = refs[8]
    for s in range(2):
        own, a, b, c = refs[4 * s : 4 * s + 4]
        total = own[...] + a[...].astype(F32) + b[...].astype(F32) + c[...].astype(F32)
        out[:, s * COLS : (s + 1) * COLS] = total.astype(BF)


def finish(parts):
    rows = parts[0].shape[0]
    tile = rows // 2
    spec = pl.BlockSpec((tile, COLS), lambda i: (i, 0))
    return pl.pallas_call(
        finish_kernel,
        out_shape=jax.ShapeDtypeStruct((rows, 2 * COLS), BF),
        grid=(2,),
        in_specs=[spec] * 8,
        out_specs=pl.BlockSpec((tile, 2 * COLS), lambda i: (i, 0)),
        compiler_params=pltpu.CompilerParams(vmem_limit_bytes=8 * MIB),
        cost_estimate=pl.CostEstimate(flops=rows * 1024, bytes_accessed=2 * MIB, transcendentals=0),
        name="finish",
    )(*parts)


def act_kernel(cot_ref, first, second, out_ref, wide):
    @pl.when(pl.program_id(0) == 0)
    def _():
        for j in range(16):
            wide[:, 256 * j : 256 * j + COLS] = first[j]
            wide[:, 256 * j + COLS : 256 * j + 256] = second[j]

    out_ref[...] = lax.dot_general(
        cot_ref[...], wide[...], (((1,), (1,)), ((), ())), preferred_element_type=F32
    ).astype(BF)


def act(cotangent, first, second):
    tokens, features = cotangent.shape
    tile = 192
    full = first.shape[1]
    spec = pl.BlockSpec((16, full, COLS), lambda i: (0, 0, 0), pipeline_mode=pl.Buffered(1))
    return pl.pallas_call(
        act_kernel,
        out_shape=jax.ShapeDtypeStruct((tokens, full), BF),
        grid=(tokens // tile,),
        in_specs=[pl.BlockSpec((tile, features), lambda i: (i, 0)), spec, spec],
        out_specs=pl.BlockSpec((tile, full), lambda i: (i, 0)),
        scratch_shapes=[pltpu.VMEM((full, features), BF)],
        compiler_params=pltpu.CompilerParams(vmem_limit_bytes=28 * MIB),
        cost_estimate=pl.CostEstimate(
            flops=2 * tokens * features * full, bytes_accessed=16 * MIB, transcendentals=0
        ),
        name="act_grad",
    )(cotangent, first, second)


def place_kernel(at, *refs):
    out = refs[-1]
    rows = refs[0].shape[0]
    for k, piece in enumerate(refs[:-1]):
        start = pl.multiple_of(((at[0] + k) % 4) * rows, rows)
        out[pl.ds(start, rows), :] = piece[...]


def gather_rows(block, axis, at):
    n = SIZE[axis]
    pieces = [block] + [shift(block, axis, -k) for k in range(1, n)]
    rows, width = block.shape
    return pl.pallas_call(
        place_kernel,
        out_shape=jax.ShapeDtypeStruct((n * rows, width), block.dtype),
        in_specs=[pl.BlockSpec(memory_space=pltpu.SMEM)] + [pl.BlockSpec(memory_space=pltpu.VMEM)] * n,
        out_specs=pl.BlockSpec(memory_space=pltpu.VMEM),
        cost_estimate=pl.CostEstimate(flops=0, bytes_accessed=8 * rows * width * 2, transcendentals=0),
        name="place",
    )(at[None].astype(jnp.int32), *pieces)


def after(value, *others):
    return lax.optimization_barrier((value, *others))[0]


def on_device(hidden, cotangent, weight, basis, first_moment, second_moment):
    zh, x, y, zl, c = (lax.axis_index(a) for a in AXES)
    tokens, full = hidden.shape

    shards = [
        lax.all_gather(weight[:, s * COLS : (s + 1) * COLS], FSDP, axis=0, tiled=False) for s in range(2)
    ]

    low_part = lax.dot_general(
        basis, hidden, (((0,), (1,)), ((), ())), preferred_element_type=F32
    ).astype(BF)
    low4 = low_part.reshape(4, 4, 32, tokens)

    def low_to(k):
        return lax.dynamic_index_in_dim(low4, (x + k) % 4, 1, keepdims=False)

    low_x = low_to(0).astype(F32)
    for k in (1, 2, 3):
        low_x = low_x + shift(low_to(k), "x", k).astype(F32)
    low_xb = low_x.astype(BF)

    def low_zto(k):
        return lax.dynamic_index_in_dim(low_xb, (zh + k) % 4, 0, keepdims=False)

    low = lax.dynamic_index_in_dim(low_x, zh, 0, keepdims=False)
    for k in (1, 2, 3):
        low = low + shift(low_zto(k), "zh", k).astype(F32)
    low = low.astype(BF)
    grad_part = jnp.dot(low, cotangent, preferred_element_type=F32)

    dests = jnp.stack([(x + k) % 4 for k in (2, 1, 3, 0)]).astype(jnp.int32)
    dests_z = jnp.stack([(zh + k) % 4 for k in (1, 2, 3, 0)]).astype(jnp.int32)

    def ring_first(pieces):
        far_up, far_down, near_up, near_down, acc_up, acc_down, own = pieces
        got_far = shift(far_up, "x", 1), shift(far_down, "x", -1)
        got_near_up, got_near_down = shift(near_up, "x", 1), shift(near_down, "x", -1)
        return add_pair(acc_up, acc_down, *got_far), (got_near_up, got_near_down)

    def ring_last(last, near):
        return shift(last[0], "x", 1), near[1], near[0], shift(last[1], "x", -1)

    def z_send(pieces):
        return [pieces[3]] + [shift(pieces[k - 1], "zh", k) for k in (1, 2, 3)]

    pieces1 = partials(after(hidden, grad_part), shards[0], dests)
    g = after(grad_part, *pieces1[:4]).reshape(32, 8, 2, 256)
    g = lax.dynamic_index_in_dim(g, c, 2, keepdims=False) + shift(
        lax.dynamic_index_in_dim(g, 1 - c, 2, keepdims=False), "c", 1
    )
    g = g.reshape(32, 4, 2, 256)
    g = lax.dynamic_index_in_dim(g, zl, 2, keepdims=False) + shift(
        lax.dynamic_index_in_dim(g, 1 - zl, 2, keepdims=False), "zl", 1
    )
    last1, near1 = ring_first(pieces1)
    grad = lax.dynamic_index_in_dim(g, y, 1, keepdims=False)
    for k in (1, 2, 3):
        grad = grad + shift(lax.dynamic_index_in_dim(g, (y + k) % 4, 1, keepdims=False), "y", k)
    new_first = 0.9 * first_moment + 0.1 * grad
    new_second = 0.999 * second_moment + 0.001 * grad * grad
    first_fix = 1.0 - 0.9**STEP
    second_fix = 1.0 - 0.999**STEP
    normed = (new_first / first_fix / (jnp.sqrt(new_second / second_fix) + 1e-08)).astype(BF)

    pieces2 = partials(after(hidden, *last1), shards[1], dests)
    normed_x = gather_rows(after(normed, *pieces2[:4]), "x", x)
    got1 = ring_last(last1, near1)
    last2, near2 = ring_first(pieces2)
    zpieces1 = regroup(pieces1[6], got1, dests_z)
    normed_all = gather_rows(after(normed_x, *zpieces1), "zh", zh)
    update = jnp.dot(basis, normed_all, preferred_element_type=F32).astype(BF)
    got2 = ring_last(last2, near2)
    act_grad = act(after(cotangent, *last2, *zpieces1), *shards)
    z1 = z_send(zpieces1)
    zpieces2 = regroup(pieces2[6], got2, dests_z)
    z2 = z_send(zpieces2)
    output = finish(z1 + z2)
    return output, act_grad, new_first, new_second, update


def solution(mesh):
    fine = Mesh(mesh.devices.reshape(tuple(SIZE[a] for a in AXES)), AXES)
    dp = ("zh", "x")
    in_specs = (
        P(FSDP, dp),
        P(FSDP, None),
        P(dp, FSDP),
        P(dp, None),
        P(dp, FSDP),
        P(dp, FSDP),
    )
    out_specs = (P(FSDP, dp), P(FSDP, dp), P(dp, FSDP), P(dp, FSDP), P(dp, FSDP))
    return jax.shard_map(
        on_device, mesh=fine, in_specs=in_specs, out_specs=out_specs, check_vma=False
    )
```

time: 371 us -> 220 us (0.59)
  the two profiles are of different devices: /device:TPU:32 before, /device:TPU:1 now
where the time goes in v1:
time: 220 us; the launch traced here: 219 us
  waiting for transfers between devices  70.1 us (32%)
  starting transfers between devices  56.5 us (26%)
  Pallas kernels  44.3 us (20%)
  local copies, waits for them, and re-layouts  23.1 us (10%)
  between operations  14.3 us (6%)
  matrix products  6.98 us (3%)
  other arithmetic  3.71 us (2%)
    ppermute x35, starting transfers between devices, shift(): return lax.ppermute(array, axis, [(i, (i + by) % n) for i in range(n)])  56.4 us
    ppermute x35, waiting for transfers between devices, shift(): return lax.ppermute(array, axis, [(i, (i + by) % n) for i in range(n)])  48.8 us
    all_gather x2, waiting for transfers between devices, on_device(): lax.all_gather(weight[:, s * COLS:(s + 1) * COLS], FSDP, axis=0, tiled=Fa...  20.6 us
    unnamed x59, local copies, waits for them, and re-layouts  15.9 us
    pallas_call x2, Pallas kernels, partials(): pl.pallas_call(functools.partial(partial_kernel, half), out_shape=[small]...  14.9 us
    pallas_call x1, Pallas kernels, act(): pl.pallas_call(act_kernel, out_shape=jax.ShapeDtypeStruct((tokens, full),...  13 us
    pallas_call x2, Pallas kernels, regroup(): pl.pallas_call(regroup_kernel, out_shape=[pltpu.HBM((rows, COLS), BF)] *...  7.27 us
  transfers between devices with their start and end apart: 37, of which 13 were waited for; matrix products, arithmetic and copies ran while one was open for 8% of the time, Pallas kernels for 19%

profile of v1, /device:TPU:1, one launch (start us, length us, event | category | flops | bytes accessed | tf_op | source)
XLA Modules:
  0.0 219.1 jit_solution(6334095223555555282)
XLA Ops:
  7.2 1.9 fusion.15
  10.0 2.4 %convolution_convert_fusion = bf16[512,768]{1,0:T(8,128)(2,1)S(1)} fusion(bf16[896,512]{1,0:T(8,128)(2,1)S(1)} %copy-done, bf16[768,896]{1,0:T(8,128)(2,1)} %h_ref.1), kind=kOutput, calls=%fused_computation | convolution fusion | flops 705036288 | bytes 3080192 | tf_op jit(solution)/shard_map/dot_general | solution.py:229
  12.4 2.1 collective-permute-start
  15.9 1.6 collective-permute-start.1
  19.6 5.7 %collective-permute-done.1 = bf16[4,32,768]{2,1,0:T(8,128)(2,1)S(1)} collective-permute-done((bf16[4,32,768]{2,1,0:T(8,128)(2,1)S(1)}, bf16[4,32,768]{2,1,0:T(8,128)(2,1)S(1)}, u32[]{:S(2)}, u32[]{:S(2)}) %collective-permute-start.1) | collective-permute-done | bytes 196640 | tf_op jit(solution)/shard_map/ppermute | solution.py:23
  25.5 3.2 %collective-permute-start.3 = (bf16[32,768]{1,0:T(8,128)(2,1)S(1)}, bf16[32,768]{1,0:T(8,128)(2,1)S(1)}, u32[]{:S(2)}, u32[]{:S(2)}) collective-permute-start(bf16[32,768]{1,0:T(8,128)(2,1)S(1)} %get-tuple-element.91), channel_id=1, source_target_pairs={{0,64},{64,128},{128,192},{192,0},{1,65},{65,129},{129,193},{193,1... | collective-permute-start | bytes 147464 | tf_op jit(solution)/shard_map/ppermute | solution.py:23
  28.7 3.1 %collective-permute-start.5 = (bf16[32,768]{1,0:T(8,128)(2,1)S(1)}, bf16[32,768]{1,0:T(8,128)(2,1)S(1)}, u32[]{:S(2)}, u32[]{:S(2)}) collective-permute-start(bf16[32,768]{1,0:T(8,128)(2,1)S(1)} %get-tuple-element.92), channel_id=1, source_target_pairs={{0,192},{64,0},{128,64},{192,128},{1,193},{65,1},{129,65},{193,129... | collective-permute-start | bytes 147464 | tf_op jit(solution)/shard_map/ppermute | solution.py:23
  31.8 4.4 %collective-permute-start.4 = (bf16[32,768]{1,0:T(8,128)(2,1)S(1)}, bf16[32,768]{1,0:T(8,128)(2,1)S(1)}, u32[]{:S(2)}, u32[]{:S(2)}) collective-permute-start(bf16[32,768]{1,0:T(8,128)(2,1)S(1)} %get-tuple-element.93), channel_id=1, source_target_pairs={{0,128},{64,192},{128,0},{192,64},{1,129},{65,193},{129,1},{193,65... | collective-permute-start | bytes 147464 | tf_op jit(solution)/shard_map/ppermute | solution.py:23
  36.3 4.1 %collective-permute-done.4 = bf16[32,768]{1,0:T(8,128)(2,1)S(1)} collective-permute-done((bf16[32,768]{1,0:T(8,128)(2,1)S(1)}, bf16[32,768]{1,0:T(8,128)(2,1)S(1)}, u32[]{:S(2)}, u32[]{:S(2)}) %collective-permute-start.4) | collective-permute-done | bytes 49184 | tf_op jit(solution)/shard_map/ppermute | solution.py:23
  40.4 4.1 %fusion.6 = f32[32,4096]{1,0:T(8,128)S(1)} fusion(bf16[768,4096]{1,0:T(8,128)(2,1)} %cot_ref, bf16[32,768]{1,0:T(8,128)(2,1)S(1)} %collective-permute-done.5, bf16[32,768]{1,0:T(8,128)(2,1)S(1)} %collective-permute-done.4, bf16[32,768]{1,0:T(8,128)(2,1)S(1)} %collective-permute-done.3, f32[4,32,768]{2,1,0:T(8,128)S(1)} %get-tuple-element.83, s32[]{:T(128)S(6)} %select_n.127), kind=kOutput, calls=%fused_computation.17 | convolution fusion | flops 201498624 | bytes 7061508 | tf_op jit(solution)/shard_map/dot_general | solution.py:249
  44.5 12.0 %all-gather.5.cloned.1.call-done = bf16[14336,128]{1,0:T(8,128)(2,1)} async-done(((bf16[896,128]{1,0:T(8,128)(2,1)}), bf16[14336,128]{1,0:T(8,128)(2,1)}) %all-gather.5.cloned.1.call-update) | async-done | bytes 3670032 | tf_op jit(solution)/shard_map/all_gather | solution.py:226
  56.5 2.0 copy-done.1
  58.6 7.4 %partials.2 = (bf16[384,512]{1,0:T(8,128)(2,1)}, bf16[384,512]{1,0:T(8,128)(2,1)}, bf16[384,512]{1,0:T(8,128)(2,1)}, bf16[384,512]{1,0:T(8,128)(2,1)}, f32[384,5...) custom-call(s32[4]{0:T(128)S(1)} %pad_add_fusion.1.pick, bf16[768,896]{1,0:T(8,128)(2,1)S(1)} %copy-done.6, ...), custom_call_target="tpu_custom_call" | custom-call | flops 2818572288 | bytes 8388608 | tf_op jit(solution)/shard_map/partials/pallas_call | solution.py:68
  67.2 1.8 constant_dynamic-slice_fusion.1
  70.1 1.6 collective-permute-done.24
  76.3 1.5 collective-permute-start.9
  77.9 3.7 %collective-permute-done.25 = f32[32,4,256]{2,0,1:T(8,128)} collective-permute-done((f32[32,4,256]{2,0,1:T(8,128)}, f32[32,4,256]{2,0,1:T(8,128)}, u32[]{:S(2)}, u32[]{:S(2)}) %collective-permute-start.25) | collective-permute-done | bytes 131104 | tf_op jit(solution)/shard_map/ppermute | solution.py:23
  83.3 1.9 collective-permute-done.6.ra
  85.2 1.4 collective-permute-start.28
  88.7 2.8 %add_pair.2 = (bf16[384,512]{1,0:T(8,128)(2,1)}, bf16[384,512]{1,0:T(8,128)(2,1)}) custom-call(f32[384,512]{1,0:T(8,128)S(1)} %copy-done.9, f32[384,512]{1,0:T(8,128)S(1)} %copy-done.10, bf16[384,512]{1,0:T(8,128)(2,1)S(1)} %collective-permute-done.6.ra, bf16[384,512]{1,0:T(8,128)(2,1)} %collective-permute-done.7.rb), custom_call_target="tpu_custom_call" | custom-call | flops 393216 | bytes 3145728 | tf_op jit(solution)/shard_map/add_pair/pallas_call | solution.py:95
  91.5 8.6 %all-gather.7.cloned.1.call-done = bf16[14336,128]{1,0:T(8,128)(2,1)} async-done(((bf16[896,128]{1,0:T(8,128)(2,1)}), bf16[14336,128]{1,0:T(8,128)(2,1)}) %all-gather.7.cloned.1.call-update) | async-done | bytes 3670032 | tf_op jit(solution)/shard_map/all_gather | solution.py:226
  100.0 2.0 copy-done.3
  102.1 7.5 %partials.3 = (bf16[384,512]{1,0:T(8,128)(2,1)}, bf16[384,512]{1,0:T(8,128)(2,1)}, bf16[384,512]{1,0:T(8,128)(2,1)}, bf16[384,512]{1,0:T(8,128)(2,1)}, f32[384,5...) custom-call(s32[4]{0:T(128)S(1)} %pad_add_fusion.1.pick, bf16[768,896]{1,0:T(8,128)(2,1)S(1)} %copy-done.6, ...), custom_call_target="tpu_custom_call" | custom-call | flops 2818572288 | bytes 8388608 | tf_op jit(solution)/shard_map/partials/pallas_call | solution.py:68
  110.4 1.8 collective-permute-start.11
  112.3 1.4 divide_convert_fusion
  113.7 2.2 collective-permute-start.30
  115.9 5.7 %collective-permute-done.31.refs_3_ = bf16[32,256]{1,0:T(8,128)(2,1)S(1)} collective-permute-done((bf16[32,256]{1,0:T(8,128)(2,1)S(1)}, bf16[32,256]{1,0:T(8,128)(2,1)S(1)}, u32[]{:S(2)}, u32[]{:S(2)}) %collective-permute-start.31) | collective-permute-done | bytes 16416 | tf_op jit(solution)/shard_map/ppermute | solution.py:23
  124.1 2.2 %collective-permute-start.16 = (bf16[384,512]{1,0:T(8,128)(2,1)}, bf16[384,512]{1,0:T(8,128)(2,1)S(1)}, u32[]{:S(2)}, u32[]{:S(2)}) collective-permute-start(bf16[384,512]{1,0:T(8,128)(2,1)} %get-tuple-element.56), channel_id=1, source_target_pairs={{0,48},{16,0},{32,16},{48,32},{1,49},{17,1},{33,17},{49,33},{2,50}... | collective-permute-start | bytes 1179656 | tf_op jit(solution)/shard_map/ppermute | solution.py:23
  126.5 1.4 place.2.refs_0_
  129.3 3.8 %regroup.2 = (bf16[768,128]{1,0:T(8,128)(2,1)}, bf16[768,128]{1,0:T(8,128)(2,1)}, bf16[768,128]{1,0:T(8,128)(2,1)}, f32[768,128]{1,0:T(8,128)}) custom-call(s32[4]{0:T(128)S(1)} %pad_add_fusion.pick, f32[768,512]{1,0:T(8,128)S(1)} %copy-done.7, bf16[384,512]{1,0:T(8,128)(2,1)S(1)} %collective-permute-done.8.last_up, ...), custom_call_target="tpu_custom_call" | custom-call | flops 3145728 | bytes 4194304 | tf_op jit(solution)/shard_map/regroup/pallas_call | solution.py:123
  133.1 2.4 %collective-permute-start.34 = (bf16[128,256]{1,0:T(8,128)(2,1)}, bf16[128,256]{1,0:T(8,128)(2,1)S(1)}, u32[]{:S(2)}, u32[]{:S(2)}) collective-permute-start(bf16[128,256]{1,0:T(8,128)(2,1)} %place.2.refs_0_), channel_id=1, source_target_pairs={{0,64},{64,128},{128,192},{192,0},{1,65},{65,129},{129,193},{193,1... | collective-permute-start | bytes 196616 | tf_op jit(solution)/shard_map/ppermute | solution.py:23
  135.5 3.5 %collective-permute-start.33 = (bf16[128,256]{1,0:T(8,128)(2,1)}, bf16[128,256]{1,0:T(8,128)(2,1)S(1)}, u32[]{:S(2)}, u32[]{:S(2)}) collective-permute-start(bf16[128,256]{1,0:T(8,128)(2,1)} %place.2.refs_0_), channel_id=1, source_target_pairs={{0,128},{64,192},{128,0},{192,64},{1,129},{65,193},{129,1},{193,65... | collective-permute-start | bytes 196616 | tf_op jit(solution)/shard_map/ppermute | solution.py:23
  139.0 2.9 %collective-permute-start.32 = (bf16[128,256]{1,0:T(8,128)(2,1)}, bf16[128,256]{1,0:T(8,128)(2,1)S(1)}, u32[]{:S(2)}, u32[]{:S(2)}) collective-permute-start(bf16[128,256]{1,0:T(8,128)(2,1)} %place.2.refs_0_), channel_id=1, source_target_pairs={{0,192},{64,0},{128,64},{192,128},{1,193},{65,1},{129,65},{193,129... | collective-permute-start | bytes 196616 | tf_op jit(solution)/shard_map/ppermute | solution.py:23
  145.7 1.5 add_pair.3
  148.5 2.1 collective-permute-start.20
  150.6 2.0 copy-done.4
  152.7 2.8 %copy-done.5 = bf16[768,4096]{1,0:T(8,128)(2,1)S(1)} copy-done((bf16[768,4096]{1,0:T(8,128)(2,1)S(1)}, bf16[768,4096]{1,0:T(8,128)(2,1)}, u32[]{:S(2)}) %copy-start.5) | copy-done | bytes 6291480
  155.5 13.0 %act_grad.1 = bf16[768,896]{1,0:T(8,128)(2,1)} custom-call(bf16[768,4096]{1,0:T(8,128)(2,1)S(1)} %copy-done.5, bf16[16,896,128]{2,1,0:T(8,128)(2,1)S(1)} %bitcast.71, bf16[16,896,128]{2,1,0:T(8,128)(2,1)S(1)} %bitcast.76), custom_call_target="tpu_custom_call" | custom-call | flops 5637144576 | bytes 16777216 | tf_op jit(solution)/shard_map/act_grad/pallas_call | solution.py:180
  168.5 1.6 place.3
  170.1 2.0 collective-permute-start.13
  172.1 1.9 collective-permute-start.14
  174.0 3.5 %regroup.3 = (bf16[768,128]{1,0:T(8,128)(2,1)}, bf16[768,128]{1,0:T(8,128)(2,1)}, bf16[768,128]{1,0:T(8,128)(2,1)}, f32[768,128]{1,0:T(8,128)}) custom-call(s32[4]{0:T(128)S(1)} %pad_add_fusion.pick, f32[768,512]{1,0:T(8,128)S(1)} %copy-done.8, bf16[384,512]{1,0:T(8,128)(2,1)} %collective-permute-done.17.last_up, ...), custom_call_target="tpu_custom_call" | custom-call | flops 3145728 | bytes 4194304 | tf_op jit(solution)/shard_map/regroup/pallas_call | solution.py:123
  177.5 1.8 collective-permute-start.21
  179.3 3.4 %collective-permute-start.22 = (bf16[768,128]{1,0:T(8,128)(2,1)}, bf16[768,128]{1,0:T(8,128)(2,1)S(1)}, u32[]{:S(2)}, u32[]{:S(2)}) collective-permute-start(bf16[768,128]{1,0:T(8,128)(2,1)} %get-tuple-element.63), channel_id=1, source_target_pairs={{0,128},{64,192},{128,0},{192,64},{1,129},{65,193},{129,1},{193,65... | collective-permute-start | bytes 589832 | tf_op jit(solution)/shard_map/ppermute | solution.py:23
  182.7 3.5 %collective-permute-start.23 = (bf16[768,128]{1,0:T(8,128)(2,1)}, bf16[768,128]{1,0:T(8,128)(2,1)S(1)}, u32[]{:S(2)}, u32[]{:S(2)}) collective-permute-start(bf16[768,128]{1,0:T(8,128)(2,1)} %get-tuple-element.64), channel_id=1, source_target_pairs={{0,192},{64,0},{128,64},{192,128},{1,193},{65,1},{129,65},{193,129... | collective-permute-start | bytes 589832 | tf_op jit(solution)/shard_map/ppermute | solution.py:23
  187.6 18.6 %collective-permute-done.14.refs_3_ = bf16[768,128]{1,0:T(8,128)(2,1)} collective-permute-done((bf16[768,128]{1,0:T(8,128)(2,1)}, bf16[768,128]{1,0:T(8,128)(2,1)}, u32[]{:S(2)}, u32[]{:S(2)}) %collective-permute-start.14) | collective-permute-done | bytes 196640 | tf_op jit(solution)/shard_map/ppermute | solution.py:23
  206.3 4.1 %collective-permute-done.23.refs_7_ = bf16[768,128]{1,0:T(8,128)(2,1)S(1)} collective-permute-done((bf16[768,128]{1,0:T(8,128)(2,1)}, bf16[768,128]{1,0:T(8,128)(2,1)S(1)}, u32[]{:S(2)}, u32[]{:S(2)}) %collective-permute-start.23) | collective-permute-done | bytes 196640 | tf_op jit(solution)/shard_map/ppermute | solution.py:23
  210.4 1.8 finish.1
  (114 shorter events, 26.7 us)
Async XLA Ops:
  7.2 49.3 %all-gather.5.cloned.1.call-start = ((), (), s32[]{:S(2)}) async-start(), calls=%async_computation | async-start | bytes 3899392 | tf_op jit(solution)/shard_map/all_gather | solution.py:226
  9.2 90.9 %all-gather.7.cloned.1.call-start = ((), (), s32[]{:S(2)}) async-start(), calls=%async_computation.1 | async-start | bytes 3899392 | tf_op jit(solution)/shard_map/all_gather | solution.py:226
  12.4 6.4 %collective-permute-start = (bf16[4,32,768]{2,1,0:T(8,128)(2,1)S(1)}, bf16[4,32,768]{2,1,0:T(8,128)(2,1)S(1)}, u32[]{:S(2)}, u32[]{:S(2)}) collective-permute-start(bf16[4,32,768]{2,1,0:T(8,128)(2,1)S(1)} %get-tuple-element.84), channel_id=1, source_target_pairs={{0,16},{16,32},{32,48},{48,0},{1,17},{17,33},{33,49},{49,1},{2,18}... | collective-permute-start | bytes 589832 | tf_op jit(solution)/shard_map/ppermute | solution.py:23
  14.5 5.1 %collective-permute-start.2 = (bf16[4,32,768]{2,1,0:T(8,128)(2,1)S(1)}, bf16[4,32,768]{2,1,0:T(8,128)(2,1)S(1)}, u32[]{:S(2)}, u32[]{:S(2)}) collective-permute-start(bf16[4,32,768]{2,1,0:T(8,128)(2,1)S(1)} %get-tuple-element.85), channel_id=1, source_target_pairs={{0,48},{16,0},{32,16},{48,32},{1,49},{17,1},{33,17},{49,33},{2,50}... | collective-permute-start | bytes 589832 | tf_op jit(solution)/shard_map/ppermute | solution.py:23
  15.9 9.5 %collective-permute-start.1 = (bf16[4,32,768]{2,1,0:T(8,128)(2,1)S(1)}, bf16[4,32,768]{2,1,0:T(8,128)(2,1)S(1)}, u32[]{:S(2)}, u32[]{:S(2)}) collective-permute-start(bf16[4,32,768]{2,1,0:T(8,128)(2,1)S(1)} %get-tuple-element.86), channel_id=1, source_target_pairs={{0,32},{16,48},{32,0},{48,16},{1,33},{17,49},{33,1},{49,17},{2,34}... | collective-permute-start | bytes 589832 | tf_op jit(solution)/shard_map/ppermute | solution.py:23
  25.5 10.8 %collective-permute-start.3 = (bf16[32,768]{1,0:T(8,128)(2,1)S(1)}, bf16[32,768]{1,0:T(8,128)(2,1)S(1)}, u32[]{:S(2)}, u32[]{:S(2)}) collective-permute-start(bf16[32,768]{1,0:T(8,128)(2,1)S(1)} %get-tuple-element.91), channel_id=1, source_target_pairs={{0,64},{64,128},{128,192},{192,0},{1,65},{65,129},{129,193},{193,1... | collective-permute-start | bytes 147464 | tf_op jit(solution)/shard_map/ppermute | solution.py:23
  28.7 7.6 %collective-permute-start.5 = (bf16[32,768]{1,0:T(8,128)(2,1)S(1)}, bf16[32,768]{1,0:T(8,128)(2,1)S(1)}, u32[]{:S(2)}, u32[]{:S(2)}) collective-permute-start(bf16[32,768]{1,0:T(8,128)(2,1)S(1)} %get-tuple-element.92), channel_id=1, source_target_pairs={{0,192},{64,0},{128,64},{192,128},{1,193},{65,1},{129,65},{193,129... | collective-permute-start | bytes 147464 | tf_op jit(solution)/shard_map/ppermute | solution.py:23
  31.8 8.6 %collective-permute-start.4 = (bf16[32,768]{1,0:T(8,128)(2,1)S(1)}, bf16[32,768]{1,0:T(8,128)(2,1)S(1)}, u32[]{:S(2)}, u32[]{:S(2)}) collective-permute-start(bf16[32,768]{1,0:T(8,128)(2,1)S(1)} %get-tuple-element.93), channel_id=1, source_target_pairs={{0,128},{64,192},{128,0},{192,64},{1,129},{65,193},{129,1},{193,65... | collective-permute-start | bytes 147464 | tf_op jit(solution)/shard_map/ppermute | solution.py:23
  40.4 16.1 %copy-start.6 = (bf16[768,896]{1,0:T(8,128)(2,1)S(1)}, bf16[768,896]{1,0:T(8,128)(2,1)}, u32[]{:S(2)}) copy-start(bf16[768,896]{1,0:T(8,128)(2,1)} %h_ref.1) | copy-start | bytes 4128772
  67.2 20.3 %copy-start.9 = (f32[384,512]{1,0:T(8,128)S(1)}, f32[384,512]{1,0:T(8,128)}, u32[]{:S(2)}) copy-start(f32[384,512]{1,0:T(8,128)} %get-tuple-element.39.a) | copy-start | bytes 2359300
  69.8 1.9 collective-permute-start.24
  73.5 8.1 %collective-permute-start.25 = (f32[32,4,256]{2,0,1:T(8,128)}, f32[32,4,256]{2,0,1:T(8,128)}, u32[]{:S(2)}, u32[]{:S(2)}) collective-permute-start(f32[32,4,256]{2,0,1:T(8,128)} %dynamic-slice_bitcast_fusion.3), channel_id=1, source_target_pairs={{0,2},{2,0},{1,3},{3,1},{4,6},{6,4},{5,7},{7,5},{8,10},{10,8},{9,1... | collective-permute-start | bytes 393224 | tf_op jit(solution)/shard_map/ppermute | solution.py:23
  73.7 11.5 %collective-permute-start.6 = (bf16[384,512]{1,0:T(8,128)(2,1)}, bf16[384,512]{1,0:T(8,128)(2,1)S(1)}, u32[]{:S(2)}, u32[]{:S(2)}) collective-permute-start(bf16[384,512]{1,0:T(8,128)(2,1)} %get-tuple-element.41), channel_id=1, source_target_pairs={{0,16},{16,32},{32,48},{48,0},{1,17},{17,33},{33,49},{49,1},{2,18}... | collective-permute-start | bytes 1179656 | tf_op jit(solution)/shard_map/ppermute | solution.py:23
  75.0 11.6 %collective-permute-start.7 = (bf16[384,512]{1,0:T(8,128)(2,1)}, bf16[384,512]{1,0:T(8,128)(2,1)}, u32[]{:S(2)}, u32[]{:S(2)}) collective-permute-start(bf16[384,512]{1,0:T(8,128)(2,1)} %get-tuple-element.42), channel_id=1, source_target_pairs={{0,48},{16,0},{32,16},{48,32},{1,49},{17,1},{33,17},{49,33},{2,50}... | collective-permute-start | bytes 1179656 | tf_op jit(solution)/shard_map/ppermute | solution.py:23
  76.3 37.4 %collective-permute-start.9 = (bf16[384,512]{1,0:T(8,128)(2,1)}, bf16[384,512]{1,0:T(8,128)(2,1)}, u32[]{:S(2)}, u32[]{:S(2)}) collective-permute-start(bf16[384,512]{1,0:T(8,128)(2,1)} %get-tuple-element.44), channel_id=1, source_target_pairs={{0,48},{16,0},{32,16},{48,32},{1,49},{17,1},{33,17},{49,33},{2,50}... | collective-permute-start | bytes 1179656 | tf_op jit(solution)/shard_map/ppermute | solution.py:23
  77.9 50.0 %collective-permute-start.10 = (bf16[384,512]{1,0:T(8,128)(2,1)}, bf16[384,512]{1,0:T(8,128)(2,1)}, u32[]{:S(2)}, u32[]{:S(2)}) collective-permute-start(bf16[384,512]{1,0:T(8,128)(2,1)} %get-tuple-element.45), channel_id=1, source_target_pairs={{0,16},{16,32},{32,48},{48,0},{1,17},{17,33},{33,49},{49,1},{2,18}... | collective-permute-start | bytes 1179656 | tf_op jit(solution)/shard_map/ppermute | solution.py:23
  83.3 26.3 %collective-permute-start.26 = (f32[32,256]{1,0:T(8,128)}, f32[32,256]{1,0:T(8,128)S(1)}, u32[]{:S(2)}, u32[]{:S(2)}) collective-permute-start(f32[32,256]{1,0:T(8,128)} %get-tuple-element.94), channel_id=1, source_target_pairs={{0,4},{4,8},{8,12},{12,0},{1,5},{5,9},{9,13},{13,1},{2,6},{6,10},{... | collective-permute-start | bytes 98312 | tf_op jit(solution)/shard_map/ppermute | solution.py:23
  85.2 25.2 %collective-permute-start.28 = (f32[32,256]{1,0:T(8,128)}, f32[32,256]{1,0:T(8,128)S(1)}, u32[]{:S(2)}, u32[]{:S(2)}) collective-permute-start(f32[32,256]{1,0:T(8,128)} %get-tuple-element.95), channel_id=1, source_target_pairs={{0,12},{4,0},{8,4},{12,8},{1,13},{5,1},{9,5},{13,9},{2,14},{6,2},{... | collective-permute-start | bytes 98312 | tf_op jit(solution)/shard_map/ppermute | solution.py:23
  86.6 25.6 %collective-permute-start.27 = (f32[32,256]{1,0:T(8,128)}, f32[32,256]{1,0:T(8,128)}, u32[]{:S(2)}, u32[]{:S(2)}) collective-permute-start(f32[32,256]{1,0:T(8,128)} %get-tuple-element.96), channel_id=1, source_target_pairs={{0,8},{4,12},{8,0},{12,4},{1,9},{5,13},{9,1},{13,5},{2,10},{6,14},... | collective-permute-start | bytes 98312 | tf_op jit(solution)/shard_map/ppermute | solution.py:23
  102.1 10.2 %copy-start.22 = (f32[32,256]{1,0:T(8,128)S(1)}, f32[32,256]{1,0:T(8,128)}, u32[]{:S(2)}) copy-start(f32[32,256]{1,0:T(8,128)} %param.11) | copy-start | bytes 98308
  102.1 10.2 %copy-start.23 = (f32[32,256]{1,0:T(8,128)S(1)}, f32[32,256]{1,0:T(8,128)}, u32[]{:S(2)}) copy-start(f32[32,256]{1,0:T(8,128)} %param.10) | copy-start | bytes 98308
  109.6 18.3 %collective-permute-start.8 = (bf16[384,512]{1,0:T(8,128)(2,1)S(1)}, bf16[384,512]{1,0:T(8,128)(2,1)S(1)}, u32[]{:S(2)}, u32[]{:S(2)}) collective-permute-start(bf16[384,512]{1,0:T(8,128)(2,1)S(1)} %copy-done.28), channel_id=1, source_target_pairs={{0,16},{16,32},{32,48},{48,0},{1,17},{17,33},{33,49},{49,1},{2,18}... | collective-permute-start | bytes 1179656 | tf_op jit(solution)/shard_map/ppermute | solution.py:23
  110.4 17.4 %collective-permute-start.11 = (bf16[384,512]{1,0:T(8,128)(2,1)S(1)}, bf16[384,512]{1,0:T(8,128)(2,1)S(1)}, u32[]{:S(2)}, u32[]{:S(2)}) collective-permute-start(bf16[384,512]{1,0:T(8,128)(2,1)S(1)} %copy-done.27), channel_id=1, source_target_pairs={{0,48},{16,0},{32,16},{48,32},{1,49},{17,1},{33,17},{49,33},{2,50}... | collective-permute-start | bytes 1179656 | tf_op jit(solution)/shard_map/ppermute | solution.py:23
  113.7 12.8 %copy-start.21 = (bf16[32,256]{1,0:T(8,128)(2,1)}, bf16[32,256]{1,0:T(8,128)(2,1)S(1)}, u32[]{:S(2)}) copy-start(bf16[32,256]{1,0:T(8,128)(2,1)S(1)} %get-tuple-element.67.refs_0_) | copy-start | bytes 49156
  113.7 7.9 %collective-permute-start.31 = (bf16[32,256]{1,0:T(8,128)(2,1)S(1)}, bf16[32,256]{1,0:T(8,128)(2,1)S(1)}, u32[]{:S(2)}, u32[]{:S(2)}) collective-permute-start(bf16[32,256]{1,0:T(8,128)(2,1)S(1)} %get-tuple-element.67.refs_0_), channel_id=1, source_target_pairs={{0,16},{16,32},{32,48},{48,0},{1,17},{17,33},{33,49},{49,1},{2,18}... | collective-permute-start | bytes 49160 | tf_op jit(solution)/shard_map/ppermute | solution.py:23
  113.7 8.9 %collective-permute-start.30 = (bf16[32,256]{1,0:T(8,128)(2,1)S(1)}, bf16[32,256]{1,0:T(8,128)(2,1)S(1)}, u32[]{:S(2)}, u32[]{:S(2)}) collective-permute-start(bf16[32,256]{1,0:T(8,128)(2,1)S(1)} %get-tuple-element.67.refs_0_), channel_id=1, source_target_pairs={{0,32},{16,48},{32,0},{48,16},{1,33},{17,49},{33,1},{49,17},{2,34}... | collective-permute-start | bytes 49160 | tf_op jit(solution)/shard_map/ppermute | solution.py:23
  121.6 2.6 %collective-permute-start.29 = (bf16[32,256]{1,0:T(8,128)(2,1)S(1)}, bf16[32,256]{1,0:T(8,128)(2,1)S(1)}, u32[]{:S(2)}, u32[]{:S(2)}) collective-permute-start(bf16[32,256]{1,0:T(8,128)(2,1)S(1)} %get-tuple-element.67.refs_0_), channel_id=1, source_target_pairs={{0,48},{16,0},{32,16},{48,32},{1,49},{17,1},{33,17},{49,33},{2,50}... | collective-permute-start | bytes 49160 | tf_op jit(solution)/shard_map/ppermute | solution.py:23
  122.6 19.4 %collective-permute-start.15 = (bf16[384,512]{1,0:T(8,128)(2,1)}, bf16[384,512]{1,0:T(8,128)(2,1)S(1)}, u32[]{:S(2)}, u32[]{:S(2)}) collective-permute-start(bf16[384,512]{1,0:T(8,128)(2,1)} %get-tuple-element.55), channel_id=1, source_target_pairs={{0,16},{16,32},{32,48},{48,0},{1,17},{17,33},{33,49},{49,1},{2,18}... | collective-permute-start | bytes 1179656 | tf_op jit(solution)/shard_map/ppermute | solution.py:23
  124.1 18.3 %collective-permute-start.16 = (bf16[384,512]{1,0:T(8,128)(2,1)}, bf16[384,512]{1,0:T(8,128)(2,1)S(1)}, u32[]{:S(2)}, u32[]{:S(2)}) collective-permute-start(bf16[384,512]{1,0:T(8,128)(2,1)} %get-tuple-element.56), channel_id=1, source_target_pairs={{0,48},{16,0},{32,16},{48,32},{1,49},{17,1},{33,17},{49,33},{2,50}... | collective-permute-start | bytes 1179656 | tf_op jit(solution)/shard_map/ppermute | solution.py:23
  129.3 21.3 %copy-start.2 = (bf16[14336,128]{1,0:T(8,128)(2,1)S(1)}, bf16[14336,128]{1,0:T(8,128)(2,1)}, u32[]{:S(2)}) copy-start(bf16[14336,128]{1,0:T(8,128)(2,1)} %all-gather.5.cloned.1.call-done) | copy-start | bytes 11010052
  133.1 14.1 %collective-permute-start.34 = (bf16[128,256]{1,0:T(8,128)(2,1)}, bf16[128,256]{1,0:T(8,128)(2,1)S(1)}, u32[]{:S(2)}, u32[]{:S(2)}) collective-permute-start(bf16[128,256]{1,0:T(8,128)(2,1)} %place.2.refs_0_), channel_id=1, source_target_pairs={{0,64},{64,128},{128,192},{192,0},{1,65},{65,129},{129,193},{193,1... | collective-permute-start | bytes 196616 | tf_op jit(solution)/shard_map/ppermute | solution.py:23
  135.5 11.7 %collective-permute-start.33 = (bf16[128,256]{1,0:T(8,128)(2,1)}, bf16[128,256]{1,0:T(8,128)(2,1)S(1)}, u32[]{:S(2)}, u32[]{:S(2)}) collective-permute-start(bf16[128,256]{1,0:T(8,128)(2,1)} %place.2.refs_0_), channel_id=1, source_target_pairs={{0,128},{64,192},{128,0},{192,64},{1,129},{65,193},{129,1},{193,65... | collective-permute-start | bytes 196616 | tf_op jit(solution)/shard_map/ppermute | solution.py:23
  139.0 8.3 %collective-permute-start.32 = (bf16[128,256]{1,0:T(8,128)(2,1)}, bf16[128,256]{1,0:T(8,128)(2,1)S(1)}, u32[]{:S(2)}, u32[]{:S(2)}) collective-permute-start(bf16[128,256]{1,0:T(8,128)(2,1)} %place.2.refs_0_), channel_id=1, source_target_pairs={{0,192},{64,0},{128,64},{192,128},{1,193},{65,1},{129,65},{193,129... | collective-permute-start | bytes 196616 | tf_op jit(solution)/shard_map/ppermute | solution.py:23
  141.9 28.2 %collective-permute-start.18 = (bf16[384,512]{1,0:T(8,128)(2,1)}, bf16[384,512]{1,0:T(8,128)(2,1)S(1)}, u32[]{:S(2)}, u32[]{:S(2)}) collective-permute-start(bf16[384,512]{1,0:T(8,128)(2,1)} %get-tuple-element.58), channel_id=1, source_target_pairs={{0,48},{16,0},{32,16},{48,32},{1,49},{17,1},{33,17},{49,33},{2,50}... | collective-permute-start | bytes 1179656 | tf_op jit(solution)/shard_map/ppermute | solution.py:23
  142.5 29.7 %collective-permute-start.19 = (bf16[384,512]{1,0:T(8,128)(2,1)}, bf16[384,512]{1,0:T(8,128)(2,1)S(1)}, u32[]{:S(2)}, u32[]{:S(2)}) collective-permute-start(bf16[384,512]{1,0:T(8,128)(2,1)} %get-tuple-element.59), channel_id=1, source_target_pairs={{0,16},{16,32},{32,48},{48,0},{1,17},{17,33},{33,49},{49,1},{2,18}... | collective-permute-start | bytes 1179656 | tf_op jit(solution)/shard_map/ppermute | solution.py:23
  147.2 21.3 %copy-start.18 = (bf16[128,256]{1,0:T(8,128)(2,1)}, bf16[128,256]{1,0:T(8,128)(2,1)S(1)}, u32[]{:S(2)}) copy-start(bf16[128,256]{1,0:T(8,128)(2,1)S(1)} %collective-permute-done.34.refs_3_) | copy-start | bytes 196612
  147.2 35.5 %collective-permute-start.12 = (bf16[768,128]{1,0:T(8,128)(2,1)}, bf16[768,128]{1,0:T(8,128)(2,1)S(1)}, u32[]{:S(2)}, u32[]{:S(2)}) collective-permute-start(bf16[768,128]{1,0:T(8,128)(2,1)} %get-tuple-element.48), channel_id=1, source_target_pairs={{0,64},{64,128},{128,192},{192,0},{1,65},{65,129},{129,193},{193,1... | collective-permute-start | bytes 589832 | tf_op jit(solution)/shard_map/ppermute | solution.py:23
  147.2 26.8 %collective-permute-start.17 = (bf16[384,512]{1,0:T(8,128)(2,1)}, bf16[384,512]{1,0:T(8,128)(2,1)}, u32[]{:S(2)}, u32[]{:S(2)}) collective-permute-start(bf16[384,512]{1,0:T(8,128)(2,1)} %get-tuple-element.57), channel_id=1, source_target_pairs={{0,16},{16,32},{32,48},{48,0},{1,17},{17,33},{33,49},{49,1},{2,18}... | collective-permute-start | bytes 1179656 | tf_op jit(solution)/shard_map/ppermute | solution.py:23
  148.5 25.5 %collective-permute-start.20 = (bf16[384,512]{1,0:T(8,128)(2,1)}, bf16[384,512]{1,0:T(8,128)(2,1)}, u32[]{:S(2)}, u32[]{:S(2)}) collective-permute-start(bf16[384,512]{1,0:T(8,128)(2,1)} %get-tuple-element.60), channel_id=1, source_target_pairs={{0,48},{16,0},{32,16},{48,32},{1,49},{17,1},{33,17},{49,33},{2,50}... | collective-permute-start | bytes 1179656 | tf_op jit(solution)/shard_map/ppermute | solution.py:23
  155.4 18.6 %copy-start.8 = (f32[768,512]{1,0:T(8,128)S(1)}, f32[768,512]{1,0:T(8,128)}, u32[]{:S(2)}) copy-start(f32[768,512]{1,0:T(8,128)} %get-tuple-element.52.own) | copy-start | bytes 4718596
  170.1 17.5 %collective-permute-start.13 = (bf16[768,128]{1,0:T(8,128)(2,1)}, bf16[768,128]{1,0:T(8,128)(2,1)}, u32[]{:S(2)}, u32[]{:S(2)}) collective-permute-start(bf16[768,128]{1,0:T(8,128)(2,1)} %get-tuple-element.49), channel_id=1, source_target_pairs={{0,128},{64,192},{128,0},{192,64},{1,129},{65,193},{129,1},{193,65... | collective-permute-start | bytes 589832 | tf_op jit(solution)/shard_map/ppermute | solution.py:23
  172.1 34.2 %collective-permute-start.14 = (bf16[768,128]{1,0:T(8,128)(2,1)}, bf16[768,128]{1,0:T(8,128)(2,1)}, u32[]{:S(2)}, u32[]{:S(2)}) collective-permute-start(bf16[768,128]{1,0:T(8,128)(2,1)} %get-tuple-element.50), channel_id=1, source_target_pairs={{0,192},{64,0},{128,64},{192,128},{1,193},{65,1},{129,65},{193,129... | collective-permute-start | bytes 589832 | tf_op jit(solution)/shard_map/ppermute | solution.py:23
  174.0 12.1 %copy-start.15 = (bf16[512,256]{1,0:T(8,128)(2,1)S(1)}, bf16[512,256]{1,0:T(8,128)(2,1)}, u32[]{:S(2)}) copy-start(bf16[512,256]{1,0:T(8,128)(2,1)} %place.3) | copy-start | bytes 786436
  177.5 32.9 %copy-start.13 = (f32[768,128]{1,0:T(8,128)S(1)}, f32[768,128]{1,0:T(8,128)}, u32[]{:S(2)}) copy-start(f32[768,128]{1,0:T(8,128)} %get-tuple-element.47.refs_0_) | copy-start | bytes 1179652
  177.5 32.9 %copy-start.14 = (f32[768,128]{1,0:T(8,128)S(1)}, f32[768,128]{1,0:T(8,128)}, u32[]{:S(2)}) copy-start(f32[768,128]{1,0:T(8,128)} %get-tuple-element.61.refs_4_) | copy-start | bytes 1179652
  177.5 28.8 %collective-permute-start.21 = (bf16[768,128]{1,0:T(8,128)(2,1)}, bf16[768,128]{1,0:T(8,128)(2,1)S(1)}, u32[]{:S(2)}, u32[]{:S(2)}) collective-permute-start(bf16[768,128]{1,0:T(8,128)(2,1)} %get-tuple-element.62), channel_id=1, source_target_pairs={{0,64},{64,128},{128,192},{192,0},{1,65},{65,129},{129,193},{193,1... | collective-permute-start | bytes 589832 | tf_op jit(solution)/shard_map/ppermute | solution.py:23
  179.3 27.0 %collective-permute-start.22 = (bf16[768,128]{1,0:T(8,128)(2,1)}, bf16[768,128]{1,0:T(8,128)(2,1)S(1)}, u32[]{:S(2)}, u32[]{:S(2)}) collective-permute-start(bf16[768,128]{1,0:T(8,128)(2,1)} %get-tuple-element.63), channel_id=1, source_target_pairs={{0,128},{64,192},{128,0},{192,64},{1,129},{65,193},{129,1},{193,65... | collective-permute-start | bytes 589832 | tf_op jit(solution)/shard_map/ppermute | solution.py:23
  182.7 27.7 %collective-permute-start.23 = (bf16[768,128]{1,0:T(8,128)(2,1)}, bf16[768,128]{1,0:T(8,128)(2,1)S(1)}, u32[]{:S(2)}, u32[]{:S(2)}) collective-permute-start(bf16[768,128]{1,0:T(8,128)(2,1)} %get-tuple-element.64), channel_id=1, source_target_pairs={{0,192},{64,0},{128,64},{192,128},{1,193},{65,1},{129,65},{193,129... | collective-permute-start | bytes 589832 | tf_op jit(solution)/shard_map/ppermute | solution.py:23
  (18 other events, 54.3 us)
Sparse Core Ops, SparseCore 0:
  10.4 46.0 all-gather.4
  58.4 41.6 all-gather.6

commit v2 on v0

v2 whole, which is shorter than its diff:
```python
import functools

import jax
import jax.numpy as jnp
from jax import lax
from jax.experimental import pallas as pl
from jax.experimental.pallas import tpu as pltpu
from jax.sharding import Mesh
from jax.sharding import PartitionSpec as P

STEP = 20
BF = jnp.bfloat16
F32 = jnp.float32
AXES = ("zh", "x", "y", "zl", "c")
SIZE = dict(zh=4, x=4, y=4, zl=2, c=2)
FSDP = ("y", "zl", "c")
DP = ("zh", "x")
W = 256
MIB = 1024 * 1024
SMALL = pl.CostEstimate(flops=1 << 20, bytes_accessed=1 << 16, transcendentals=0)


def shift(array, axis, by):
    n = SIZE[axis]
    return lax.ppermute(array, axis, [(i, (i + by) % n) for i in range(n)])


def swap(array, axes):
    return lax.all_to_all(array, axes, 0, 0, tiled=True)


def after(value, *others):
    return lax.optimization_barrier((value, *others))[0]


def in_hbm(value):
    return pltpu.with_memory_space_constraint(value, pltpu.HBM)


def params(limit):
    return pltpu.CompilerParams(vmem_limit_bytes=limit * MIB)


def partial_kernel(m, slot_of, h_ref, *refs):
    w_refs, outs, wide = refs[: 4 * m], refs[4 * m : 4 * m + 4], refs[4 * m + 4]
    k = pl.program_id(0)
    for slot in range(4):

        @pl.when(slot_of[k] == slot)
        def _(slot=slot):
            for block in range(m):
                wide[:, block * W : (block + 1) * W] = w_refs[4 * block + slot][...]

    product = jnp.dot(h_ref[...], wide[...], preferred_element_type=F32).astype(BF)
    for which in range(4):

        @pl.when(k == which)
        def _(which=which):
            outs[which][...] = product


def partials(hidden, blocks, slot_of, start, rows):
    full = hidden.shape[1]
    m = len(blocks)
    flat = [w for four in blocks for w in four]
    return pl.pallas_call(
        functools.partial(partial_kernel, m),
        out_shape=[pltpu.HBM((rows, m * W), BF)] * 4,
        grid_spec=pltpu.PrefetchScalarGridSpec(
            num_scalar_prefetch=1,
            grid=(4,),
            in_specs=[pl.BlockSpec((rows, full), lambda n, s: (start // rows, 0))]
            + [pl.BlockSpec((full, W), lambda n, s: (0, 0), pipeline_mode=pl.Buffered(1))] * (4 * m),
            out_specs=[pl.BlockSpec((rows, m * W), lambda n, s: (0, 0))] * 4,
            scratch_shapes=[pltpu.VMEM((full, m * W), BF)],
        ),
        compiler_params=params(20),
        cost_estimate=SMALL,
        name="partials",
    )(slot_of, in_hbm(hidden), *flat)


def regroup_kernel(offsets, place, *refs):
    out = refs[-1]
    for s, offs in enumerate(offsets):
        four = refs[4 * s : 4 * s + 4]
        total = four[0][...].astype(F32)
        for ref in four[1:]:
            total += ref[...].astype(F32)
        total = total.astype(BF)
        for block, off in enumerate(offs):
            out[place[off]] = total[:, block * W : (block + 1) * W]


def regroup(first, second, offsets, place, start, rows):
    tile = rows // 2
    return pl.pallas_call(
        functools.partial(regroup_kernel, offsets),
        out_shape=pltpu.HBM((4, rows, W), BF),
        grid_spec=pltpu.PrefetchScalarGridSpec(
            num_scalar_prefetch=1,
            grid=(2,),
            in_specs=[pl.BlockSpec((tile, W), lambda i, s: (start // tile + i, 0))] * 4
            + [pl.BlockSpec((tile, 3 * W), lambda i, s: (i, 0))] * 4,
            out_specs=pl.BlockSpec((4, tile, W), lambda i, s: (0, i, 0)),
        ),
        compiler_params=params(16),
        cost_estimate=SMALL,
        name="regroup",
    )(place, *first, *second)


def x_reduce(parts):
    return [parts[3]] + [shift(parts[k - 1], "x", k) for k in (1, 3, 2)]


def finish_kernel(first, second, out):
    i = pl.program_id(0)
    for which, ref in enumerate((first, second)):

        @pl.when(i == which)
        def _(ref=ref):
            total = ref[0].astype(F32)
            for s in range(1, 4):
                total += ref[s].astype(F32)
            out[...] = total.astype(BF)


def finish(first, second):
    rows = first.shape[1]
    spec = pl.BlockSpec((4, rows, W), lambda i: (0, 0, 0))
    return pl.pallas_call(
        finish_kernel,
        out_shape=jax.ShapeDtypeStruct((2 * rows, W), BF),
        grid=(2,),
        in_specs=[spec] * 2,
        out_specs=pl.BlockSpec((rows, W), lambda i: (i, 0)),
        compiler_params=params(12),
        cost_estimate=SMALL,
        name="finish",
    )(first, second)


def act_kernel(order, cot_ref, *refs):
    w_refs, out_ref, wide = refs[:16], refs[16], refs[17]

    @pl.when(pl.program_id(0) == 0)
    def _():
        for s in range(16):
            wide[:, pl.ds(pl.multiple_of(order[s] * W, W), W)] = w_refs[s][...]

    out_ref[...] = lax.dot_general(
        cot_ref[...], wide[...], (((1,), (1,)), ((), ())), preferred_element_type=F32
    ).astype(BF)


def act(cotangent, shards, order):
    tokens, features = cotangent.shape
    tile = tokens // 2
    full = shards[0].shape[0]
    spec = pl.BlockSpec((full, W), lambda i, s: (0, 0), pipeline_mode=pl.Buffered(1))
    return pl.pallas_call(
        act_kernel,
        out_shape=jax.ShapeDtypeStruct((tokens, full), BF),
        grid_spec=pltpu.PrefetchScalarGridSpec(
            num_scalar_prefetch=1,
            grid=(tokens // tile,),
            in_specs=[pl.BlockSpec((tile, features), lambda i, s: (i, 0))] + [spec] * 16,
            out_specs=pl.BlockSpec((tile, full), lambda i, s: (i, 0)),
            scratch_shapes=[pltpu.VMEM((full, features), BF)],
        ),
        compiler_params=params(32),
        cost_estimate=SMALL,
        name="act_grad",
    )(order, in_hbm(cotangent), *shards)


def on_device(hidden, cotangent, weight, basis, first_moment, second_moment):
    zh, x, y, zl, c = (lax.axis_index(a) for a in AXES)
    tokens = hidden.shape[0]
    half = tokens // 2

    side = shift(weight, "zl", 1)
    next0, prev0 = shift(weight, "y", -1), shift(weight, "y", 1)
    next1, prev1 = shift(side, "y", -1), shift(side, "y", 1)
    far0 = shift(after(next0, next1), "y", -1)
    far1 = shift(prev1, "y", 1)
    held = {0: (weight, side), 1: (next0, next1), 3: (prev0, prev1), 2: (far0, far1)}
    slots = {
        off: (own, shift(own, "c", 1), other, shift(other, "c", 1)) for off, (own, other) in held.items()
    }
    dest = [2 * (zl ^ (s // 2)) + (c ^ (s % 2)) for s in range(4)]
    goals = [(x + k) % 4 for k in (1, 2, 3, 0)]
    slot_of = jnp.stack([2 * ((g // 2) ^ zl) + ((g % 2) ^ c) for g in goals]).astype(jnp.int32)
    place = jnp.stack([(y + k) % 4 for k in range(4)]).astype(jnp.int32)

    low_part = lax.dot_general(
        basis, hidden, (((0,), (1,)), ((), ())), preferred_element_type=F32
    ).astype(BF)
    low_all = swap(low_part.reshape(16, 32, tokens), DP)

    part0 = partials(after(hidden, next0, prev0), [slots[0]], slot_of, 0, tokens)
    sum0 = x_reduce(part0)

    low = jnp.sum(after(low_all, *part0).astype(F32), axis=0).astype(BF)
    grad_part = jnp.dot(low, cotangent, preferred_element_type=F32)
    grad_all = swap(grad_part.reshape(32, 16, W).transpose(1, 0, 2), FSDP)

    others = (1, 3, 2)
    kept = {off: [in_hbm(w) for w in four] for off, four in slots.items()}
    rest = [kept[off] for off in others]
    part1 = partials(after(hidden, grad_part, *sum0[1:]), rest, slot_of, 0, half)
    sum1 = x_reduce(part1)

    grad = jnp.sum(after(grad_all, *part1), axis=0)
    new_first = 0.9 * first_moment + 0.1 * grad
    new_second = 0.999 * second_moment + 0.001 * grad * grad
    first_fix = 1.0 - 0.9**STEP
    second_fix = 1.0 - 0.999**STEP
    normed = (new_first / first_fix / (jnp.sqrt(new_second / second_fix) + 1e-08)).astype(BF)
    normed_all = swap(jnp.broadcast_to(normed[None], (16, *normed.shape)), DP)

    part2 = partials(after(hidden, *part1), rest, slot_of, half, half)
    sum2 = x_reduce(lax.optimization_barrier((*part2, *sum1[1:]))[:4])

    order, shards = [], []
    for off, four in kept.items():
        for slot, w in enumerate(four):
            order.append(((y + off) % 4) * 4 + dest[slot])
            shards.append(w)
    act_grad = act(after(cotangent, *part2), shards, jnp.stack(order).astype(jnp.int32))
    offsets = ((0,), others)
    zpart1 = regroup(sum0, sum1, offsets, after(place, act_grad, *part2), 0, half)
    normed_all = after(normed_all, zpart1).reshape(-1, W)
    update = jnp.dot(basis, normed_all, preferred_element_type=F32).astype(BF)
    got1 = swap(zpart1, "zh")
    got2 = swap(regroup(sum0, sum2, offsets, place, half, half), "zh")
    output = finish(got1, got2)
    return output, act_grad, new_first, new_second, update


def solution(mesh):
    fine = Mesh(mesh.devices.reshape(tuple(SIZE[a] for a in AXES)), AXES)
    in_specs = (
        P(FSDP, DP),
        P(FSDP, None),
        P(DP, FSDP),
        P(DP, None),
        P(DP, FSDP),
        P(DP, FSDP),
    )
    out_specs = (P(FSDP, DP), P(FSDP, DP), P(DP, FSDP), P(DP, FSDP), P(DP, FSDP))
    return jax.shard_map(
        on_device, mesh=fine, in_specs=in_specs, out_specs=out_specs, check_vma=False
    )
```

time: 371 us -> 209 us (0.56)
  blocking collectives: 169 us -> 0 us
  starting transfers between devices: 0.12 us -> 64 us
  waiting for transfers between devices: 146 us -> 82.7 us
  Pallas kernels: 0 us -> 42.1 us
  matrix products: 31.6 us -> 8.64 us
  between operations: 13.8 us -> 0.92 us
  local copies, waits for them, and re-layouts: 1.55 us -> 6.24 us
    reduce_scatter x2 -> x0, waiting for transfers between devices: 146 us -> none  [the longest x1 98.1 us: on_device(): lax.psum_scatter(partial_out, 'dp', scatter_dimension=1, tiled=True)]
    psum x1 -> x0, blocking collectives: 117 us -> none  [on_device(): low_whole = lax.psum(low_part, 'dp').astype(jnp.bfloat16)]
    ppermute x0 -> x24, waiting for transfers between devices: none -> 66.1 us  [shift(): return lax.ppermute(array, axis, [(i, (i + by) % n) for i in range(n)])]
    all_gather x1 -> x0, blocking collectives: 51.9 us -> none  [on_device(): normed_all = lax.all_gather(normed, 'dp', axis=0, tiled=True)]
    pallas_call x0 -> x7, Pallas kernels: none -> 42.1 us  [the longest x3 23.1 us: partials(): pl.pallas_call(functools.partial(partial_kernel, m), out_shape=[pltpu.HBM...]
    all_to_all x0 -> x5, starting transfers between devices: none -> 36.8 us  [swap(): return lax.all_to_all(array, axes, 0, 0, tiled=True)]
    ppermute x0 -> x24, starting transfers between devices: none -> 27.2 us  [shift(): return lax.ppermute(array, axis, [(i, (i + by) % n) for i in range(n)])]
    dot_general x5 -> x3, matrix products: 31.6 us -> 8.64 us  [the longest x1 3.97 us: on_device(): grad_part = jnp.dot(low, cotangent, preferred_element_type=F32)]
  transfers between devices with their start and end apart: 3 -> 29, of which waited for: 2 -> 10; matrix products, arithmetic and copies ran while one was open for 9% -> 5% of each run, Pallas kernels for 0% -> 20%
where the time goes in v2:
time: 209 us; the launch traced here: 208 us
  waiting for transfers between devices  82.7 us (40%)
  starting transfers between devices  64 us (31%)
  Pallas kernels  42.1 us (20%)
  matrix products  8.64 us (4%)
  local copies, waits for them, and re-layouts  6.24 us (3%)
  other arithmetic  3.12 us (1%)
    ppermute x24, waiting for transfers between devices, shift(): return lax.ppermute(array, axis, [(i, (i + by) % n) for i in range(n)])  66.1 us
    all_to_all x5, starting transfers between devices, swap(): return lax.all_to_all(array, axes, 0, 0, tiled=True)  36.8 us
    ppermute x24, starting transfers between devices, shift(): return lax.ppermute(array, axis, [(i, (i + by) % n) for i in range(n)])  27.2 us
    pallas_call x3, Pallas kernels, partials(): pl.pallas_call(functools.partial(partial_kernel, m), out_shape=[pltpu.HBM...  23.1 us
    all_to_all x5, waiting for transfers between devices, swap(): return lax.all_to_all(array, axes, 0, 0, tiled=True)  16.6 us
    pallas_call x1, Pallas kernels, act(): pl.pallas_call(act_kernel, out_shape=jax.ShapeDtypeStruct((tokens, full),...  13.4 us
    pallas_call x2, Pallas kernels, regroup(): pl.pallas_call(functools.partial(regroup_kernel, offsets), out_shape=pltp...  4.72 us
    unnamed x37, local copies, waits for them, and re-layouts  4.56 us
  transfers between devices with their start and end apart: 29, of which 10 were waited for; matrix products, arithmetic and copies ran while one was open for 5% of the time, Pallas kernels for 20%

profile of v2, /device:TPU:32, one launch (start us, length us, event | category | flops | bytes accessed | tf_op | source)
XLA Modules:
  0.0 207.8 jit_solution(4269123385004282897)
XLA Ops:
  0.6 1.2 copy-done
  1.8 3.2 %convolution_convert_fusion = bf16[512,768]{1,0:T(8,128)(2,1)} fusion(bf16[896,512]{1,0:T(8,128)(2,1)S(1)} %copy-done, bf16[768,896]{1,0:T(8,128)(2,1)} %h_ref.2), kind=kOutput, calls=%fused_computation | convolution fusion | flops 705036288 | bytes 3080192 | tf_op jit(solution)/shard_map/dot_general | solution.py:197
  5.1 10.3 %all-to-all-start = ((bf16[16,32,768]{2,1,0:T(8,128)(2,1)}), bf16[16,32,768]{2,1,0:T(8,128)(2,1)}, u32[]{:S(2)}, u32[]{:S(2)}) async-start(bf16[16,32,768]{2,1,0:T(8,128)(2,1)} %bitcast.24), calls=%async_computation | async-start | bytes 1572864 | tf_op jit(solution)/shard_map/all_to_all | solution.py:29
  15.4 1.1 collective-permute-start.3
  16.5 1.6 collective-permute-start.1
  18.1 1.7 collective-permute-start
  19.7 23.9 %collective-permute-done.3.refs_2_ = bf16[896,256]{1,0:T(8,128)(2,1)S(1)} collective-permute-done((bf16[896,256]{1,0:T(8,128)(2,1)S(1)}, bf16[896,256]{1,0:T(8,128)(2,1)S(1)}, u32[]{:S(2)}, u32[]{:S(2)}) %collective-permute-start.3) | collective-permute-done | bytes 458784 | tf_op jit(solution)/shard_map/ppermute | solution.py:25
  43.7 1.6 collective-permute-start.12
  45.4 1.7 collective-permute-start.9
  47.2 5.7 %partials.3 = (bf16[768,256]{1,0:T(8,128)(2,1)}, bf16[768,256]{1,0:T(8,128)(2,1)}, bf16[768,256]{1,0:T(8,128)(2,1)}, bf16[768,256]{1,0:T(8,128)(2,1)}) custom-call(s32[4]{0:T(128)S(1)} %pad_add_fusion.1.slot_of, bf16[768,896]{1,0:T(8,128)(2,1)} %h_ref.2, bf16[896,256]{1,0:T(8,128)(2,1)S(1)} %copy-done.1, ...), custom_call_target="tpu_custom_call" | custom-call | flops 1048576 | bytes 65536 | tf_op jit(solution)/shard_map/partials/pallas_call | solution.py:66
  52.9 1.2 reduce_sum.21
  54.2 4.0 %fusion.3 = f32[32,4096]{1,0:T(8,128)S(1)} fusion(bf16[32,768]{1,0:T(8,128)(2,1)S(1)} %reduce_sum.21, bf16[768,4096]{1,0:T(8,128)(2,1)} %cot_ref), kind=kOutput, calls=%fused_computation.10 | convolution fusion | flops 201326592 | bytes 6864896 | tf_op jit(solution)/shard_map/dot_general | solution.py:206
  58.1 0.9 copy.16
  59.0 5.0 %all-to-all-start.3 = ((f32[16,32,256]{2,1,0:T(8,128)}), f32[16,32,256]{2,1,0:T(8,128)}, u32[]{:S(2)}, u32[]{:S(2)}) async-start(f32[16,32,256]{2,1,0:T(8,128)} %bitcast.40), calls=%async_computation.3 | async-start | bytes 1048576 | tf_op jit(solution)/shard_map/all_to_all | solution.py:29
  64.0 1.6 collective-permute-start.16
  65.6 1.7 collective-permute-start.14
  67.3 1.7 collective-permute-start.5
  69.1 2.7 %collective-permute-start.7 = (bf16[768,256]{1,0:T(8,128)(2,1)}, bf16[768,256]{1,0:T(8,128)(2,1)S(1)}, u32[]{:S(2)}, u32[]{:S(2)}) collective-permute-start(bf16[768,256]{1,0:T(8,128)(2,1)} %get-tuple-element.32), channel_id=1, source_target_pairs={{0,32},{16,48},{32,0},{48,16},{1,33},{17,49},{33,1},{49,17},{2,34}... | collective-permute-start | bytes 1179656 | tf_op jit(solution)/shard_map/ppermute | solution.py:25
  71.8 1.4 collective-permute-start.6
  73.2 6.4 %collective-permute-done.5.refs_1_ = bf16[768,256]{1,0:T(8,128)(2,1)S(1)} collective-permute-done((bf16[768,256]{1,0:T(8,128)(2,1)}, bf16[768,256]{1,0:T(8,128)(2,1)S(1)}, u32[]{:S(2)}, u32[]{:S(2)}) %collective-permute-start.5) | collective-permute-done | bytes 393248 | tf_op jit(solution)/shard_map/ppermute | solution.py:25
  79.6 9.4 %collective-permute-done.7.refs_3_ = bf16[768,256]{1,0:T(8,128)(2,1)S(1)} collective-permute-done((bf16[768,256]{1,0:T(8,128)(2,1)}, bf16[768,256]{1,0:T(8,128)(2,1)S(1)}, u32[]{:S(2)}, u32[]{:S(2)}) %collective-permute-start.7) | collective-permute-done | bytes 393248 | tf_op jit(solution)/shard_map/ppermute | solution.py:25
  90.0 1.0 collective-permute-done.13.refs_7_.refs_11_
  91.0 1.3 collective-permute-done.10.refs_3_.refs_7_
  93.2 0.8 copy-done.15
  94.1 8.7 %partials.4 = (bf16[384,768]{1,0:T(8,128)(2,1)}, bf16[384,768]{1,0:T(8,128)(2,1)}, bf16[384,768]{1,0:T(8,128)(2,1)}, bf16[384,768]{1,0:T(8,128)(2,1)}) custom-call(s32[4]{0:T(128)S(1)} %pad_add_fusion.1.slot_of, bf16[768,896]{1,0:T(8,128)(2,1)} %h_ref.2, bf16[896,256]{1,0:T(8,128)(2,1)} %collective-permute-done.refs_0_.refs_4_, bf16[896,256]{1,0:T(8,128)(2,1)} %copy-done.11, ...), custom_call_target="tpu_custom_call" | custom-call | flops 1048576 | bytes 65536 | tf_op jit(solution)/shard_map/partials/pallas_call | solution.py:66
  102.9 2.4 %collective-permute-start.20 = (bf16[384,768]{1,0:T(8,128)(2,1)}, bf16[384,768]{1,0:T(8,128)(2,1)}, u32[]{:S(2)}, u32[]{:S(2)}) collective-permute-start(bf16[384,768]{1,0:T(8,128)(2,1)} %get-tuple-element.39), channel_id=1, source_target_pairs={{0,32},{16,48},{32,0},{48,16},{1,33},{17,49},{33,1},{49,17},{2,34}... | collective-permute-start | bytes 1769480 | tf_op jit(solution)/shard_map/ppermute | solution.py:25
  105.2 1.8 collective-permute-start.19
  107.0 1.1 reduce_sum.22
  108.1 0.6 divide_convert_fusion
  108.8 0.7 broadcast_in_dim.2
  109.5 7.6 %all-to-all-start.4 = ((bf16[16,32,256]{2,1,0:T(8,128)(2,1)}), bf16[16,32,256]{2,1,0:T(8,128)(2,1)}, u32[]{:S(2)}, u32[]{:S(2)}) async-start(bf16[16,32,256]{2,1,0:T(8,128)(2,1)} %broadcast_in_dim.2), calls=%async_computation.4 | async-start | bytes 524288 | tf_op jit(solution)/shard_map/all_to_all | solution.py:29
  117.4 8.7 %partials.5 = (bf16[384,768]{1,0:T(8,128)(2,1)}, bf16[384,768]{1,0:T(8,128)(2,1)}, bf16[384,768]{1,0:T(8,128)(2,1)}, bf16[384,768]{1,0:T(8,128)(2,1)}) custom-call(s32[4]{0:T(128)S(1)} %pad_add_fusion.1.slot_of, bf16[768,896]{1,0:T(8,128)(2,1)} %h_ref.2, bf16[896,256]{1,0:T(8,128)(2,1)} %collective-permute-done.refs_0_.refs_4_, bf16[896,256]{1,0:T(8,128)(2,1)} %copy-done.11, ...), custom_call_target="tpu_custom_call" | custom-call | flops 1048576 | bytes 65536 | tf_op jit(solution)/shard_map/partials/pallas_call | solution.py:66
  126.1 13.4 %act_grad.1 = bf16[768,896]{1,0:T(8,128)(2,1)} custom-call(s32[16]{0:T(128)S(1)} %stack.102.order, bf16[768,4096]{1,0:T(8,128)(2,1)} %cot_ref, bf16[896,256]{1,0:T(8,128)(2,1)} %refs_0_.3, bf16[896,256]{1,0:T(8,128)(2,1)} %copy-done.3, bf16[896,256]{1,0:T(8,128)(2,1)} %copy-done.2, bf16[896,256]{1,0:T(8,128)(2,1)} %copy-done.4, ...), custom_call_target="tpu_custom_call" | custom-call | flops 1048576 | bytes 65536 | tf_op jit(solution)/shard_map/act_grad/pallas_call | solution.py:162
  139.5 3.0 %regroup.2 = bf16[4,384,256]{2,1,0:T(8,128)(2,1)} custom-call(s32[4]{0:T(128)S(1)} %pad_add_fusion.place, bf16[768,256]{1,0:T(8,128)(2,1)S(1)} %copy-done.5, bf16[768,256]{1,0:T(8,128)(2,1)S(1)} %collective-permute-done.5.refs_1_, bf16[768,256]{1,0:T(8,128)(2,1)S(1)} %collective-permute-done.6.refs_2_, bf16[768,256]{1,0:T(8,128)(2,1)S(1)} %collective-permute-done.7.refs_3_, ...), custom_call_target="tpu_custom_call" | custom-call | flops 1048576 | bytes 65536 | tf_op jit(solution)/shard_map/regroup/pallas_call | solution.py:97
  142.5 7.0 %all-to-all-start.1 = ((bf16[4,384,256]{2,1,0:T(8,128)(2,1)}), bf16[4,384,256]{2,1,0:T(8,128)(2,1)S(1)}, u32[]{:S(2)}, u32[]{:S(2)}) async-start(bf16[4,384,256]{2,1,0:T(8,128)(2,1)} %regroup.2), calls=%async_computation.1 | async-start | bytes 1572864 | tf_op jit(solution)/shard_map/all_to_all | solution.py:29
  149.5 1.5 collective-permute-start.21
  151.0 1.8 collective-permute-start.22
  152.7 1.8 collective-permute-start.23
  154.5 11.8 %collective-permute-done.21.refs_5_ = bf16[384,768]{1,0:T(8,128)(2,1)S(1)} collective-permute-done((bf16[384,768]{1,0:T(8,128)(2,1)}, bf16[384,768]{1,0:T(8,128)(2,1)S(1)}, u32[]{:S(2)}, u32[]{:S(2)}) %collective-permute-start.21) | collective-permute-done | bytes 589856 | tf_op jit(solution)/shard_map/ppermute | solution.py:25
  166.3 10.4 %collective-permute-done.22.refs_6_ = bf16[384,768]{1,0:T(8,128)(2,1)S(1)} collective-permute-done((bf16[384,768]{1,0:T(8,128)(2,1)}, bf16[384,768]{1,0:T(8,128)(2,1)S(1)}, u32[]{:S(2)}, u32[]{:S(2)}) %collective-permute-start.22) | collective-permute-done | bytes 589856 | tf_op jit(solution)/shard_map/ppermute | solution.py:25
  176.6 1.5 collective-permute-done.23.refs_7_
  178.1 1.1 copy-done.7
  179.2 1.8 regroup.3
  181.0 6.9 %all-to-all-start.2 = ((bf16[4,384,256]{2,1,0:T(8,128)(2,1)}), bf16[4,384,256]{2,1,0:T(8,128)(2,1)S(1)}, u32[]{:S(2)}, u32[]{:S(2)}) async-start(bf16[4,384,256]{2,1,0:T(8,128)(2,1)} %regroup.3), calls=%async_computation.2 | async-start | bytes 1572864 | tf_op jit(solution)/shard_map/all_to_all | solution.py:29
  187.9 1.4 fusion
  189.3 1.0 copy.13
  190.3 16.6 %all-to-all-done.2.second = bf16[4,384,256]{2,1,0:T(8,128)(2,1)S(1)} async-done(((bf16[4,384,256]{2,1,0:T(8,128)(2,1)}), bf16[4,384,256]{2,1,0:T(8,128)(2,1)S(1)}, u32[]{:S(2)}, u32[]{:S(2)}) %all-to-all-start.2) | async-done | bytes 786464 | tf_op jit(solution)/shard_map/all_to_all | solution.py:29
  206.9 0.9 finish.1
  (65 shorter events, 2.5 us)
Async XLA Ops:
  0.6 1.2 copy-start
  5.1 10.3 %copy-start.1 = (bf16[896,256]{1,0:T(8,128)(2,1)S(1)}, bf16[896,256]{1,0:T(8,128)(2,1)}, u32[]{:S(2)}) copy-start(bf16[896,256]{1,0:T(8,128)(2,1)} %refs_0_.3) | copy-start | bytes 1376260
  5.1 47.9 %all-to-all-start = ((bf16[16,32,768]{2,1,0:T(8,128)(2,1)}), bf16[16,32,768]{2,1,0:T(8,128)(2,1)}, u32[]{:S(2)}, u32[]{:S(2)}) async-start(bf16[16,32,768]{2,1,0:T(8,128)(2,1)} %bitcast.24), calls=%async_computation | async-start | bytes 1572864 | tf_op jit(solution)/shard_map/all_to_all | solution.py:29
  15.4 28.2 %collective-permute-start.3 = (bf16[896,256]{1,0:T(8,128)(2,1)S(1)}, bf16[896,256]{1,0:T(8,128)(2,1)S(1)}, u32[]{:S(2)}, u32[]{:S(2)}) collective-permute-start(bf16[896,256]{1,0:T(8,128)(2,1)S(1)} %copy-done.1), channel_id=1, source_target_pairs={{0,2},{2,0},{1,3},{3,1},{4,6},{6,4},{5,7},{7,5},{8,10},{10,8},{9,1... | collective-permute-start | bytes 1376264 | tf_op jit(solution)/shard_map/ppermute | solution.py:25
  16.5 27.2 %collective-permute-start.1 = (bf16[896,256]{1,0:T(8,128)(2,1)S(1)}, bf16[896,256]{1,0:T(8,128)(2,1)S(1)}, u32[]{:S(2)}, u32[]{:S(2)}) collective-permute-start(bf16[896,256]{1,0:T(8,128)(2,1)S(1)} %copy-done.1), channel_id=1, source_target_pairs={{0,4},{4,8},{8,12},{12,0},{1,5},{5,9},{9,13},{13,1},{2,6},{6,10},{... | collective-permute-start | bytes 1376264 | tf_op jit(solution)/shard_map/ppermute | solution.py:25
  18.1 25.7 %collective-permute-start = (bf16[896,256]{1,0:T(8,128)(2,1)S(1)}, bf16[896,256]{1,0:T(8,128)(2,1)}, u32[]{:S(2)}, u32[]{:S(2)}) collective-permute-start(bf16[896,256]{1,0:T(8,128)(2,1)S(1)} %copy-done.1), channel_id=1, source_target_pairs={{0,12},{4,0},{8,4},{12,8},{1,13},{5,1},{9,5},{13,9},{2,14},{6,2},{... | collective-permute-start | bytes 1376264 | tf_op jit(solution)/shard_map/ppermute | solution.py:25
  19.7 27.4 %collective-permute-start.2 = (bf16[896,256]{1,0:T(8,128)(2,1)S(1)}, bf16[896,256]{1,0:T(8,128)(2,1)S(1)}, u32[]{:S(2)}, u32[]{:S(2)}) collective-permute-start(bf16[896,256]{1,0:T(8,128)(2,1)S(1)} %copy-done.1), channel_id=1, source_target_pairs={{0,1},{1,0},{2,3},{3,2},{4,5},{5,4},{6,7},{7,6},{8,9},{9,8},{10,11... | collective-permute-start | bytes 1376264 | tf_op jit(solution)/shard_map/ppermute | solution.py:25
  43.6 9.3 %copy-start.2 = (bf16[896,256]{1,0:T(8,128)(2,1)}, bf16[896,256]{1,0:T(8,128)(2,1)S(1)}, u32[]{:S(2)}) copy-start(bf16[896,256]{1,0:T(8,128)(2,1)S(1)} %collective-permute-done.3.refs_2_) | copy-start | bytes 1376260
  43.6 3.5 %collective-permute-start.4 = (bf16[896,256]{1,0:T(8,128)(2,1)S(1)}, bf16[896,256]{1,0:T(8,128)(2,1)S(1)}, u32[]{:S(2)}, u32[]{:S(2)}) collective-permute-start(bf16[896,256]{1,0:T(8,128)(2,1)S(1)} %collective-permute-done.3.refs_2_), channel_id=1, source_target_pairs={{0,1},{1,0},{2,3},{3,2},{4,5},{5,4},{6,7},{7,6},{8,9},{9,8},{10,11... | collective-permute-start | bytes 1376264 | tf_op jit(solution)/shard_map/ppermute | solution.py:25
  43.7 9.2 %copy-start.8 = (bf16[896,256]{1,0:T(8,128)(2,1)}, bf16[896,256]{1,0:T(8,128)(2,1)S(1)}, u32[]{:S(2)}) copy-start(bf16[896,256]{1,0:T(8,128)(2,1)S(1)} %collective-permute-done.1.refs_4_.refs_8_) | copy-start | bytes 1376260
  43.7 20.3 %collective-permute-start.12 = (bf16[896,256]{1,0:T(8,128)(2,1)S(1)}, bf16[896,256]{1,0:T(8,128)(2,1)}, u32[]{:S(2)}, u32[]{:S(2)}) collective-permute-start(bf16[896,256]{1,0:T(8,128)(2,1)S(1)} %collective-permute-done.3.refs_2_), channel_id=1, source_target_pairs={{0,4},{4,8},{8,12},{12,0},{1,5},{5,9},{9,13},{13,1},{2,6},{6,10},{... | collective-permute-start | bytes 1376264 | tf_op jit(solution)/shard_map/ppermute | solution.py:25
  45.4 18.6 %collective-permute-start.9 = (bf16[896,256]{1,0:T(8,128)(2,1)S(1)}, bf16[896,256]{1,0:T(8,128)(2,1)}, u32[]{:S(2)}, u32[]{:S(2)}) collective-permute-start(bf16[896,256]{1,0:T(8,128)(2,1)S(1)} %collective-permute-done.3.refs_2_), channel_id=1, source_target_pairs={{0,12},{4,0},{8,4},{12,8},{1,13},{5,1},{9,5},{13,9},{2,14},{6,2},{... | collective-permute-start | bytes 1376264 | tf_op jit(solution)/shard_map/ppermute | solution.py:25
  47.1 24.7 %collective-permute-start.11 = (bf16[896,256]{1,0:T(8,128)(2,1)S(1)}, bf16[896,256]{1,0:T(8,128)(2,1)}, u32[]{:S(2)}, u32[]{:S(2)}) collective-permute-start(bf16[896,256]{1,0:T(8,128)(2,1)S(1)} %collective-permute-done.1.refs_4_.refs_8_), channel_id=1, source_target_pairs={{0,1},{1,0},{2,3},{3,2},{4,5},{5,4},{6,7},{7,6},{8,9},{9,8},{10,11... | collective-permute-start | bytes 1376264 | tf_op jit(solution)/shard_map/ppermute | solution.py:25
  47.1 5.8 %copy-start.3 = (bf16[896,256]{1,0:T(8,128)(2,1)}, bf16[896,256]{1,0:T(8,128)(2,1)S(1)}, u32[]{:S(2)}) copy-start(bf16[896,256]{1,0:T(8,128)(2,1)S(1)} %collective-permute-done.2.refs_1_) | copy-start | bytes 1376260
  47.1 5.8 %copy-start.4 = (bf16[896,256]{1,0:T(8,128)(2,1)}, bf16[896,256]{1,0:T(8,128)(2,1)S(1)}, u32[]{:S(2)}) copy-start(bf16[896,256]{1,0:T(8,128)(2,1)S(1)} %collective-permute-done.4.refs_3_) | copy-start | bytes 1376260
  59.0 48.0 %all-to-all-start.3 = ((f32[16,32,256]{2,1,0:T(8,128)}), f32[16,32,256]{2,1,0:T(8,128)}, u32[]{:S(2)}, u32[]{:S(2)}) async-start(f32[16,32,256]{2,1,0:T(8,128)} %bitcast.40), calls=%async_computation.3 | async-start | bytes 1048576 | tf_op jit(solution)/shard_map/all_to_all | solution.py:29
  64.0 44.1 %copy-start.16 = (f32[32,256]{1,0:T(8,128)S(1)}, f32[32,256]{1,0:T(8,128)}, u32[]{:S(2)}) copy-start(f32[32,256]{1,0:T(8,128)} %param.11) | copy-start | bytes 98308
  64.0 44.1 %copy-start.17 = (f32[32,256]{1,0:T(8,128)S(1)}, f32[32,256]{1,0:T(8,128)}, u32[]{:S(2)}) copy-start(f32[32,256]{1,0:T(8,128)} %param.10) | copy-start | bytes 98308
  64.0 25.5 %collective-permute-start.16 = (bf16[896,256]{1,0:T(8,128)(2,1)}, bf16[896,256]{1,0:T(8,128)(2,1)S(1)}, u32[]{:S(2)}, u32[]{:S(2)}) collective-permute-start(bf16[896,256]{1,0:T(8,128)(2,1)} %collective-permute-done.12.refs_6_.refs_10_), channel_id=1, source_target_pairs={{0,4},{4,8},{8,12},{12,0},{1,5},{5,9},{9,13},{13,1},{2,6},{6,10},{... | collective-permute-start | bytes 1376264 | tf_op jit(solution)/shard_map/ppermute | solution.py:25
  65.6 24.0 %collective-permute-start.14 = (bf16[896,256]{1,0:T(8,128)(2,1)}, bf16[896,256]{1,0:T(8,128)(2,1)S(1)}, u32[]{:S(2)}, u32[]{:S(2)}) collective-permute-start(bf16[896,256]{1,0:T(8,128)(2,1)} %collective-permute-done.refs_0_.refs_4_), channel_id=1, source_target_pairs={{0,12},{4,0},{8,4},{12,8},{1,13},{5,1},{9,5},{13,9},{2,14},{6,2},{... | collective-permute-start | bytes 1376264 | tf_op jit(solution)/shard_map/ppermute | solution.py:25
  67.3 12.3 %collective-permute-start.5 = (bf16[768,256]{1,0:T(8,128)(2,1)}, bf16[768,256]{1,0:T(8,128)(2,1)S(1)}, u32[]{:S(2)}, u32[]{:S(2)}) collective-permute-start(bf16[768,256]{1,0:T(8,128)(2,1)} %get-tuple-element.31), channel_id=1, source_target_pairs={{0,16},{16,32},{32,48},{48,0},{1,17},{17,33},{33,49},{49,1},{2,18}... | collective-permute-start | bytes 1179656 | tf_op jit(solution)/shard_map/ppermute | solution.py:25
  69.1 19.9 %collective-permute-start.7 = (bf16[768,256]{1,0:T(8,128)(2,1)}, bf16[768,256]{1,0:T(8,128)(2,1)S(1)}, u32[]{:S(2)}, u32[]{:S(2)}) collective-permute-start(bf16[768,256]{1,0:T(8,128)(2,1)} %get-tuple-element.32), channel_id=1, source_target_pairs={{0,32},{16,48},{32,0},{48,16},{1,33},{17,49},{33,1},{49,17},{2,34}... | collective-permute-start | bytes 1179656 | tf_op jit(solution)/shard_map/ppermute | solution.py:25
  71.8 17.2 %collective-permute-start.6 = (bf16[768,256]{1,0:T(8,128)(2,1)}, bf16[768,256]{1,0:T(8,128)(2,1)S(1)}, u32[]{:S(2)}, u32[]{:S(2)}) collective-permute-start(bf16[768,256]{1,0:T(8,128)(2,1)} %get-tuple-element.33), channel_id=1, source_target_pairs={{0,48},{16,0},{32,16},{48,32},{1,49},{17,1},{33,17},{49,33},{2,50}... | collective-permute-start | bytes 1179656 | tf_op jit(solution)/shard_map/ppermute | solution.py:25
  79.6 10.4 %collective-permute-start.8 = (bf16[896,256]{1,0:T(8,128)(2,1)}, bf16[896,256]{1,0:T(8,128)(2,1)S(1)}, u32[]{:S(2)}, u32[]{:S(2)}) collective-permute-start(bf16[896,256]{1,0:T(8,128)(2,1)} %collective-permute-done.refs_0_.refs_4_), channel_id=1, source_target_pairs={{0,1},{1,0},{2,3},{3,2},{4,5},{5,4},{6,7},{7,6},{8,9},{9,8},{10,11... | collective-permute-start | bytes 1376264 | tf_op jit(solution)/shard_map/ppermute | solution.py:25
  89.0 2.0 collective-permute-start.13
  89.0 3.3 %collective-permute-start.10 = (bf16[896,256]{1,0:T(8,128)(2,1)}, bf16[896,256]{1,0:T(8,128)(2,1)S(1)}, u32[]{:S(2)}, u32[]{:S(2)}) collective-permute-start(bf16[896,256]{1,0:T(8,128)(2,1)} %collective-permute-done.9.refs_2_.refs_6_), channel_id=1, source_target_pairs={{0,1},{1,0},{2,3},{3,2},{4,5},{5,4},{6,7},{7,6},{8,9},{9,8},{10,11... | collective-permute-start | bytes 1376264 | tf_op jit(solution)/shard_map/ppermute | solution.py:25
  89.5 3.3 %copy-start.9 = (bf16[896,256]{1,0:T(8,128)(2,1)}, bf16[896,256]{1,0:T(8,128)(2,1)S(1)}, u32[]{:S(2)}) copy-start(bf16[896,256]{1,0:T(8,128)(2,1)S(1)} %collective-permute-done.16.refs_10_.refs_14_) | copy-start | bytes 1376260
  89.5 2.8 %collective-permute-start.17 = (bf16[896,256]{1,0:T(8,128)(2,1)S(1)}, bf16[896,256]{1,0:T(8,128)(2,1)S(1)}, u32[]{:S(2)}, u32[]{:S(2)}) collective-permute-start(bf16[896,256]{1,0:T(8,128)(2,1)S(1)} %collective-permute-done.16.refs_10_.refs_14_), channel_id=1, source_target_pairs={{0,1},{1,0},{2,3},{3,2},{4,5},{5,4},{6,7},{7,6},{8,9},{9,8},{10,11... | collective-permute-start | bytes 1376264 | tf_op jit(solution)/shard_map/ppermute | solution.py:25
  89.6 3.2 %copy-start.10 = (bf16[896,256]{1,0:T(8,128)(2,1)}, bf16[896,256]{1,0:T(8,128)(2,1)S(1)}, u32[]{:S(2)}) copy-start(bf16[896,256]{1,0:T(8,128)(2,1)S(1)} %collective-permute-done.14.refs_8_.refs_12_) | copy-start | bytes 1376260
  89.6 3.2 %collective-permute-start.15 = (bf16[896,256]{1,0:T(8,128)(2,1)S(1)}, bf16[896,256]{1,0:T(8,128)(2,1)S(1)}, u32[]{:S(2)}, u32[]{:S(2)}) collective-permute-start(bf16[896,256]{1,0:T(8,128)(2,1)S(1)} %collective-permute-done.14.refs_8_.refs_12_), channel_id=1, source_target_pairs={{0,1},{1,0},{2,3},{3,2},{4,5},{5,4},{6,7},{7,6},{8,9},{9,8},{10,11... | collective-permute-start | bytes 1376264 | tf_op jit(solution)/shard_map/ppermute | solution.py:25
  90.0 2.8 %copy-start.11 = (bf16[896,256]{1,0:T(8,128)(2,1)}, bf16[896,256]{1,0:T(8,128)(2,1)S(1)}, u32[]{:S(2)}) copy-start(bf16[896,256]{1,0:T(8,128)(2,1)S(1)} %collective-permute-done.8.refs_1_.refs_5_) | copy-start | bytes 1376260
  91.0 1.8 copy-start.12
  92.3 0.8 copy-start.13
  92.3 0.9 copy-start.14
  93.2 0.8 copy-start.15
  102.7 36.7 %collective-permute-start.18 = (bf16[384,768]{1,0:T(8,128)(2,1)}, bf16[384,768]{1,0:T(8,128)(2,1)}, u32[]{:S(2)}, u32[]{:S(2)}) collective-permute-start(bf16[384,768]{1,0:T(8,128)(2,1)} %get-tuple-element.38), channel_id=1, source_target_pairs={{0,16},{16,32},{32,48},{48,0},{1,17},{17,33},{33,49},{49,1},{2,18}... | collective-permute-start | bytes 1769480 | tf_op jit(solution)/shard_map/ppermute | solution.py:25
  102.9 36.6 %collective-permute-start.20 = (bf16[384,768]{1,0:T(8,128)(2,1)}, bf16[384,768]{1,0:T(8,128)(2,1)}, u32[]{:S(2)}, u32[]{:S(2)}) collective-permute-start(bf16[384,768]{1,0:T(8,128)(2,1)} %get-tuple-element.39), channel_id=1, source_target_pairs={{0,32},{16,48},{32,0},{48,16},{1,33},{17,49},{33,1},{49,17},{2,34}... | collective-permute-start | bytes 1769480 | tf_op jit(solution)/shard_map/ppermute | solution.py:25
  105.2 34.2 %collective-permute-start.19 = (bf16[384,768]{1,0:T(8,128)(2,1)}, bf16[384,768]{1,0:T(8,128)(2,1)}, u32[]{:S(2)}, u32[]{:S(2)}) collective-permute-start(bf16[384,768]{1,0:T(8,128)(2,1)} %get-tuple-element.40), channel_id=1, source_target_pairs={{0,48},{16,0},{32,16},{48,32},{1,49},{17,1},{33,17},{49,33},{2,50}... | collective-permute-start | bytes 1769480 | tf_op jit(solution)/shard_map/ppermute | solution.py:25
  109.5 33.0 %all-to-all-start.4 = ((bf16[16,32,256]{2,1,0:T(8,128)(2,1)}), bf16[16,32,256]{2,1,0:T(8,128)(2,1)}, u32[]{:S(2)}, u32[]{:S(2)}) async-start(bf16[16,32,256]{2,1,0:T(8,128)(2,1)} %broadcast_in_dim.2), calls=%async_computation.4 | async-start | bytes 524288 | tf_op jit(solution)/shard_map/all_to_all | solution.py:29
  126.1 13.4 %copy-start.5 = (bf16[768,256]{1,0:T(8,128)(2,1)S(1)}, bf16[768,256]{1,0:T(8,128)(2,1)}, u32[]{:S(2)}) copy-start(bf16[768,256]{1,0:T(8,128)(2,1)} %get-tuple-element.34.refs_0_) | copy-start | bytes 1179652
  126.1 13.4 %copy-start.6 = (bf16[384,768]{1,0:T(8,128)(2,1)S(1)}, bf16[384,768]{1,0:T(8,128)(2,1)}, u32[]{:S(2)}) copy-start(bf16[384,768]{1,0:T(8,128)(2,1)} %get-tuple-element.41.refs_4_) | copy-start | bytes 1769476
  142.5 38.5 %all-to-all-start.1 = ((bf16[4,384,256]{2,1,0:T(8,128)(2,1)}), bf16[4,384,256]{2,1,0:T(8,128)(2,1)S(1)}, u32[]{:S(2)}, u32[]{:S(2)}) async-start(bf16[4,384,256]{2,1,0:T(8,128)(2,1)} %regroup.2), calls=%async_computation.1 | async-start | bytes 1572864 | tf_op jit(solution)/shard_map/all_to_all | solution.py:29
  149.5 16.8 %collective-permute-start.21 = (bf16[384,768]{1,0:T(8,128)(2,1)}, bf16[384,768]{1,0:T(8,128)(2,1)S(1)}, u32[]{:S(2)}, u32[]{:S(2)}) collective-permute-start(bf16[384,768]{1,0:T(8,128)(2,1)} %get-tuple-element.50), channel_id=1, source_target_pairs={{0,16},{16,32},{32,48},{48,0},{1,17},{17,33},{33,49},{49,1},{2,18}... | collective-permute-start | bytes 1769480 | tf_op jit(solution)/shard_map/ppermute | solution.py:25
  151.0 25.7 %collective-permute-start.22 = (bf16[384,768]{1,0:T(8,128)(2,1)}, bf16[384,768]{1,0:T(8,128)(2,1)S(1)}, u32[]{:S(2)}, u32[]{:S(2)}) collective-permute-start(bf16[384,768]{1,0:T(8,128)(2,1)} %get-tuple-element.51), channel_id=1, source_target_pairs={{0,48},{16,0},{32,16},{48,32},{1,49},{17,1},{33,17},{49,33},{2,50}... | collective-permute-start | bytes 1769480 | tf_op jit(solution)/shard_map/ppermute | solution.py:25
  152.7 25.4 %collective-permute-start.23 = (bf16[384,768]{1,0:T(8,128)(2,1)}, bf16[384,768]{1,0:T(8,128)(2,1)S(1)}, u32[]{:S(2)}, u32[]{:S(2)}) collective-permute-start(bf16[384,768]{1,0:T(8,128)(2,1)} %get-tuple-element.52), channel_id=1, source_target_pairs={{0,32},{16,48},{32,0},{48,16},{1,33},{17,49},{33,1},{49,17},{2,34}... | collective-permute-start | bytes 1769480 | tf_op jit(solution)/shard_map/ppermute | solution.py:25
  178.1 1.1 copy-start.7
  181.0 25.9 %all-to-all-start.2 = ((bf16[4,384,256]{2,1,0:T(8,128)(2,1)}), bf16[4,384,256]{2,1,0:T(8,128)(2,1)S(1)}, u32[]{:S(2)}, u32[]{:S(2)}) async-start(bf16[4,384,256]{2,1,0:T(8,128)(2,1)} %regroup.3), calls=%async_computation.2 | async-start | bytes 1572864 | tf_op jit(solution)/shard_map/all_to_all | solution.py:29

commit v3 on v2

v3 whole, which is shorter than its diff:
```python
import functools

import jax
import jax.numpy as jnp
from jax import lax
from jax.experimental import pallas as pl
from jax.experimental.pallas import tpu as pltpu
from jax.sharding import Mesh
from jax.sharding import PartitionSpec as P

STEP = 20
BF = jnp.bfloat16
F32 = jnp.float32
AXES = ("zh", "x", "y", "zl", "c")
SIZE = dict(zh=4, x=4, y=4, zl=2, c=2)
FSDP = ("y", "zl", "c")
DP = ("zh", "x")
W = 256
MIB = 1024 * 1024
LIGHT = pl.CostEstimate(flops=1 << 20, bytes_accessed=1 << 16, transcendentals=0)
COST = pl.CostEstimate(flops=1 << 33, bytes_accessed=1 << 25, transcendentals=0)


def shift(array, axis, by):
    n = SIZE[axis]
    return lax.ppermute(array, axis, [(i, (i + by) % n) for i in range(n)])


def swap(array, axes):
    return lax.all_to_all(array, axes, 0, 0, tiled=True)


def after(value, *others):
    return lax.optimization_barrier((value, *others))[0]


def in_hbm(value):
    return pltpu.with_memory_space_constraint(value, pltpu.HBM)


def params(limit):
    return pltpu.CompilerParams(vmem_limit_bytes=limit * MIB)


def partial_kernel(m, slot_of, h_ref, *refs):
    w_refs, outs = refs[: 4 * m], refs[4 * m : 4 * m + 4]
    wide, held, w_sems, out_sems = refs[4 * m + 4 :]

    def fetch(k):
        for block in range(m):
            for slot in range(4):

                @pl.when(slot_of[k] == slot)
                def _(block=block, slot=slot):
                    load(k, block, slot).start()

    def load(k, block, slot):
        return pltpu.make_async_copy(
            w_refs[4 * block + slot],
            wide.at[k % 2, :, pl.ds(block * W, W)],
            w_sems.at[k % 2, block],
        )

    def store(k):
        return pltpu.make_async_copy(held.at[k % 2], outs[k], out_sems.at[k % 2])

    fetch(0)
    fetch(1)
    for k in range(4):
        for block in range(m):
            load(k, block, 0).wait()
        if k >= 2:
            store(k - 2).wait()
        held[k % 2] = jnp.dot(h_ref[...], wide[k % 2], preferred_element_type=F32).astype(BF)
        store(k).start()
        if k < 2:
            fetch(k + 2)
    store(2).wait()
    store(3).wait()


def partials(hidden, blocks, slot_of, start, rows):
    full = hidden.shape[1]
    m = len(blocks)
    flat = [w for four in blocks for w in four]
    return pl.pallas_call(
        functools.partial(partial_kernel, m),
        out_shape=[pltpu.HBM((rows, m * W), BF)] * 4,
        grid_spec=pltpu.PrefetchScalarGridSpec(
            num_scalar_prefetch=1,
            grid=(1,),
            in_specs=[pl.BlockSpec((rows, full), lambda n, s: (start // rows, 0))]
            + [pl.BlockSpec(memory_space=pl.ANY)] * (4 * m),
            out_specs=[pl.BlockSpec(memory_space=pl.ANY)] * 4,
            scratch_shapes=[
                pltpu.VMEM((2, full, m * W), BF),
                pltpu.VMEM((2, rows, m * W), BF),
                pltpu.SemaphoreType.DMA((2, m)),
                pltpu.SemaphoreType.DMA((2,)),
            ],
        ),
        compiler_params=params(14),
        cost_estimate=COST,
        name="partials",
    )(slot_of, in_hbm(hidden), *flat)


def regroup_kernel(offsets, place, *refs):
    outs = refs[8:]
    for s, offs in enumerate(offsets):
        four = refs[4 * s : 4 * s + 4]
        total = four[0][...].astype(F32)
        for ref in four[1:]:
            total += ref[...].astype(F32)
        total = total.astype(BF)
        for block, off in enumerate(offs):
            for which in range(4):

                @pl.when(place[off] == which)
                def _(total=total, block=block, which=which):
                    outs[which][...] = total[:, block * W : (block + 1) * W]


def regroup(first, second, offsets, place, start, rows):
    tile = rows // 2
    return pl.pallas_call(
        functools.partial(regroup_kernel, offsets),
        out_shape=[pltpu.HBM((rows, W), BF)] * 4,
        grid_spec=pltpu.PrefetchScalarGridSpec(
            num_scalar_prefetch=1,
            grid=(2,),
            in_specs=[pl.BlockSpec((tile, W), lambda i, s: (start // tile + i, 0))] * 4
            + [pl.BlockSpec((tile, 3 * W), lambda i, s: (i, 0))] * 4,
            out_specs=[pl.BlockSpec((tile, W), lambda i, s: (i, 0))] * 4,
        ),
        compiler_params=params(16),
        cost_estimate=COST,
        name="regroup",
    )(place, *first, *second)


def spread(parts, axis):
    got = [parts[3]] + [shift(parts[k - 1], axis, k) for k in (1, 3, 2)]
    return [in_hbm(part) for part in got] if axis == "x" else got


def finish_kernel(*refs):
    i = pl.program_id(0)
    out = refs[8]
    for which in range(2):

        @pl.when(i == which)
        def _(which=which):
            four = refs[4 * which : 4 * which + 4]
            total = four[0][...].astype(F32)
            for ref in four[1:]:
                total += ref[...].astype(F32)
            out[...] = total.astype(BF)


def finish(first, second):
    rows = first[0].shape[0]
    spec = pl.BlockSpec((rows, W), lambda i: (0, 0))
    return pl.pallas_call(
        finish_kernel,
        out_shape=jax.ShapeDtypeStruct((2 * rows, W), BF),
        grid=(2,),
        in_specs=[spec] * 8,
        out_specs=pl.BlockSpec((rows, W), lambda i: (i, 0)),
        compiler_params=params(12),
        cost_estimate=LIGHT,
        name="finish",
    )(*first, *second)


def low_kernel(parts, out):
    total = parts[0].astype(F32)
    for s in range(1, 4):
        total += parts[s].astype(F32)
    out[...] = total.astype(BF)


def low_sum(parts):
    return pl.pallas_call(
        low_kernel,
        out_shape=jax.ShapeDtypeStruct(parts.shape[1:], BF),
        in_specs=[pl.BlockSpec(memory_space=pltpu.VMEM)],
        out_specs=pl.BlockSpec(memory_space=pltpu.VMEM),
        compiler_params=params(8),
        cost_estimate=COST,
        name="low_sum",
    )(parts)


def grad_kernel(low_ref, cot_ref, out, low):
    @pl.when(pl.program_id(0) == 0)
    def _():
        low_kernel(low_ref, low)

    for block in range(4):
        out[block] = jnp.dot(
            low[...], cot_ref[:, block * W : (block + 1) * W], preferred_element_type=F32
        )


def grad_partial(low_parts, cotangent):
    tokens, features = cotangent.shape
    ranks = low_parts.shape[1]
    return pl.pallas_call(
        grad_kernel,
        out_shape=pltpu.HBM((features // W, ranks, W), F32),
        grid=(features // (4 * W),),
        in_specs=[
            pl.BlockSpec(low_parts.shape, lambda i: (0, 0, 0)),
            pl.BlockSpec((tokens, 4 * W), lambda i: (0, i)),
        ],
        out_specs=pl.BlockSpec((4, ranks, W), lambda i: (i, 0, 0)),
        scratch_shapes=[pltpu.VMEM((ranks, tokens), BF)],
        compiler_params=params(8),
        cost_estimate=COST,
        name="grad_partial",
    )(low_parts, in_hbm(cotangent))


def moments_kernel(grads, first, second, new_first, new_second, normed):
    grad = grads[0]
    for s in range(1, 16):
        grad = grad + grads[s]
    one = 0.9 * first[...] + 0.1 * grad
    two = 0.999 * second[...] + 0.001 * grad * grad
    new_first[...] = one
    new_second[...] = two
    first_fix = 1.0 - 0.9**STEP
    second_fix = 1.0 - 0.999**STEP
    step = (one / first_fix / (jnp.sqrt(two / second_fix) + 1e-08)).astype(BF)
    for s in range(16):
        normed[s] = step


def moments(grads, first, second):
    full = pl.BlockSpec(memory_space=pltpu.VMEM)
    return pl.pallas_call(
        moments_kernel,
        out_shape=[jax.ShapeDtypeStruct(first.shape, F32)] * 2
        + [jax.ShapeDtypeStruct((16, *first.shape), BF)],
        in_specs=[full] * 3,
        out_specs=[full] * 3,
        compiler_params=params(8),
        cost_estimate=LIGHT,
        name="moments",
    )(grads, first, second)


def act_kernel(order, cot_ref, *refs):
    w_refs, out_ref, wide = refs[:16], refs[16], refs[17]

    @pl.when(pl.program_id(0) == 0)
    def _():
        for s in range(16):
            wide[:, pl.ds(pl.multiple_of(order[s] * W, W), W)] = w_refs[s][...]

    out_ref[...] = lax.dot_general(
        cot_ref[...], wide[...], (((1,), (1,)), ((), ())), preferred_element_type=F32
    ).astype(BF)


def act(cotangent, shards, order):
    tokens, features = cotangent.shape
    tile = tokens // 2
    full = shards[0].shape[0]
    spec = pl.BlockSpec((full, W), lambda i, s: (0, 0), pipeline_mode=pl.Buffered(1))
    return pl.pallas_call(
        act_kernel,
        out_shape=jax.ShapeDtypeStruct((tokens, full), BF),
        grid_spec=pltpu.PrefetchScalarGridSpec(
            num_scalar_prefetch=1,
            grid=(tokens // tile,),
            in_specs=[pl.BlockSpec((tile, features), lambda i, s: (i, 0))] + [spec] * 16,
            out_specs=pl.BlockSpec((tile, full), lambda i, s: (i, 0)),
            scratch_shapes=[pltpu.VMEM((full, features), BF)],
        ),
        compiler_params=params(32),
        cost_estimate=COST,
        name="act_grad",
    )(order, in_hbm(cotangent), *shards)


def on_device(hidden, cotangent, weight, basis, first_moment, second_moment):
    zh, x, y, zl, c = (lax.axis_index(a) for a in AXES)
    tokens = hidden.shape[0]
    half = tokens // 2

    low_part = lax.dot_general(
        basis, hidden, (((0,), (1,)), ((), ())), preferred_element_type=F32
    ).astype(BF)
    low_part = low_part.reshape(4, 4, 32, tokens).transpose(1, 0, 2, 3)

    side = shift(weight, "zl", 1)
    next0, prev0 = shift(weight, "y", -1), shift(weight, "y", 1)
    low_x = swap(after(low_part, weight), "x")
    side = after(side, low_part, next0, prev0)
    next1, prev1 = shift(side, "y", -1), shift(side, "y", 1)

    def both_cores(own, other):
        return own, shift(own, "c", 1), other, shift(other, "c", 1)

    dest = [2 * (zl ^ (s // 2)) + (c ^ (s % 2)) for s in range(4)]
    goals = [(x + k) % 4 for k in (1, 2, 3, 0)]
    slot_of = jnp.stack([2 * ((g // 2) ^ zl) + ((g % 2) ^ c) for g in goals]).astype(jnp.int32)
    place = jnp.stack([(y + k - zh + 3) % 4 for k in range(4)]).astype(jnp.int32)

    slots = {0: both_cores(weight, side)}
    part0 = partials(after(hidden, next0, prev0, low_x), [slots[0]], slot_of, 0, tokens)
    sum0 = spread(part0, "x")
    far0 = shift(after(next0, next1, *part0), "y", -1)
    far1 = shift(after(prev1, *part0), "y", 1)
    slots[1] = both_cores(next0, next1)
    slots[3] = both_cores(prev0, prev1)
    slots[2] = both_cores(after(far0, *sum0[1:]), after(far1, *sum0[1:]))

    low_x = low_sum(after(low_x, *part0))
    low_z = swap(low_x, "zh")

    others = (1, 3, 2)
    kept = {off: [in_hbm(w) for w in four] for off, four in slots.items()}
    rest = [kept[off] for off in others]
    part1 = partials(after(hidden, low_x), rest, slot_of, 0, half)
    sum1 = spread(part1, "x")

    part2 = partials(after(hidden, *part1), rest, slot_of, half, half)
    grad_all = swap(grad_partial(after(low_z, *part2), cotangent), FSDP)

    sum2 = spread(lax.optimization_barrier((*part2, *sum1[1:]))[:4], "x")
    offsets = ((0,), others)
    zpart1 = regroup(sum0, sum1, offsets, after(place, *part2), 0, half)
    got1 = spread(zpart1, "zh")

    new_first, new_second, normed = moments(after(grad_all, *zpart1), first_moment, second_moment)
    normed_all = swap(normed, DP)

    order, shards = [], []
    for off, four in kept.items():
        for slot, w in enumerate(four):
            order.append(((y + off) % 4) * 4 + dest[slot])
            shards.append(w)
    zpart2 = regroup(sum0, sum2, offsets, after(place, *zpart1), half, half)
    got2 = spread(zpart2, "zh")
    act_grad = act(after(cotangent, *zpart2), shards, jnp.stack(order).astype(jnp.int32))
    normed_all = after(normed_all, *zpart2).reshape(-1, W)
    update = jnp.dot(basis, normed_all, preferred_element_type=F32).astype(BF)
    output = finish(got1, got2)
    return output, act_grad, new_first, new_second, update


def solution(mesh):
    fine = Mesh(mesh.devices.reshape(tuple(SIZE[a] for a in AXES)), AXES)
    in_specs = (
        P(FSDP, DP),
        P(FSDP, None),
        P(DP, FSDP),
        P(DP, None),
        P(DP, FSDP),
        P(DP, FSDP),
    )
    out_specs = (P(FSDP, DP), P(FSDP, DP), P(DP, FSDP), P(DP, FSDP), P(DP, FSDP))
    return jax.shard_map(
        on_device, mesh=fine, in_specs=in_specs, out_specs=out_specs, check_vma=False
    )
```

time: 209 us -> 170 us (0.81)
  waiting for transfers between devices: 82.7 us -> 41.7 us
  Pallas kernels: 42.1 us -> 51.9 us
  matrix products: 8.64 us -> 2.84 us
  starting transfers between devices: 64 us -> 67.7 us
  other arithmetic: 3.12 us -> 0.16 us
  local copies, waits for them, and re-layouts: 6.24 us -> 3.78 us
    ppermute x24 -> x30, waiting for transfers between devices: 66.1 us -> 36.2 us  [shift(): return lax.ppermute(array, axis, [(i, (i + by) % n) for i in range(n)])]
    ppermute x24 -> x30, starting transfers between devices: 27.2 us -> 42.5 us  [shift(): return lax.ppermute(array, axis, [(i, (i + by) % n) for i in range(n)])]
    all_to_all x5 -> x4, starting transfers between devices: 36.8 us -> 25.3 us  [swap(): return lax.all_to_all(array, axes, 0, 0, tiled=True)]
    all_to_all x5 -> x4, waiting for transfers between devices: 16.6 us -> 5.48 us  [swap(): return lax.all_to_all(array, axes, 0, 0, tiled=True)]
    pallas_call x2 -> x5, Pallas kernels: 4.72 us -> 13.9 us  [the longest x2 7.27 us: regroup(): pl.pallas_call(functools.partial(regroup_kernel, offsets), out_shape=[plt...]
    dot_general x1 -> x0, matrix products: 3.97 us -> none  [on_device(): grad_part = jnp.dot(low, cotangent, preferred_element_type=F32)]
    reduce_sum x2 -> x0, other arithmetic: 2.33 us -> none  [the longest x1 1.25 us: on_device(): low = jnp.sum(after(low_all, *part0).astype(F32), axis=0).astype(BF)]
    unnamed x37 -> x35, local copies, waits for them, and re-layouts: 4.56 us -> 2.76 us
  transfers between devices with their start and end apart: 29 -> 34, of which waited for: 10 -> 10; matrix products, arithmetic and copies ran while one was open for 5% -> 2% of each run, Pallas kernels for 20% -> 31%
where the time goes in v3:
time: 170 us; the launch traced here: 169 us
  starting transfers between devices  67.7 us (40%)
  Pallas kernels  51.9 us (31%)
  waiting for transfers between devices  41.7 us (25%)
  local copies, waits for them, and re-layouts  3.78 us (2%)
  matrix products  2.84 us (2%)
    ppermute x30, starting transfers between devices, shift(): return lax.ppermute(array, axis, [(i, (i + by) % n) for i in range(n)])  42.5 us
    ppermute x30, waiting for transfers between devices, shift(): return lax.ppermute(array, axis, [(i, (i + by) % n) for i in range(n)])  36.2 us
    all_to_all x4, starting transfers between devices, swap(): return lax.all_to_all(array, axes, 0, 0, tiled=True)  25.3 us
    pallas_call x3, Pallas kernels, partials(): pl.pallas_call(functools.partial(partial_kernel, m), out_shape=[pltpu.HBM...  23.7 us
    pallas_call x1, Pallas kernels, act(): pl.pallas_call(act_kernel, out_shape=jax.ShapeDtypeStruct((tokens, full),...  13.3 us
    pallas_call x2, Pallas kernels, regroup(): pl.pallas_call(functools.partial(regroup_kernel, offsets), out_shape=[plt...  7.27 us
    all_to_all x4, waiting for transfers between devices, swap(): return lax.all_to_all(array, axes, 0, 0, tiled=True)  5.48 us
    pallas_call x1, Pallas kernels, grad_partial(): pl.pallas_call(grad_kernel, out_shape=pltpu.HBM((features // W, ranks, W)...  5.12 us
  transfers between devices with their start and end apart: 34, of which 10 were waited for; matrix products, arithmetic and copies ran while one was open for 2% of the time, Pallas kernels for 31%

profile of v3, /device:TPU:32, one launch (start us, length us, event | category | flops | bytes accessed | tf_op | source)
XLA Modules:
  0.0 169.1 jit_solution(14049525097058078698)
XLA Ops:
  0.6 1.9 %collective-permute-start.3 = (bf16[896,256]{1,0:T(8,128)(2,1)}, bf16[896,256]{1,0:T(8,128)(2,1)S(1)}, u32[]{:S(2)}, u32[]{:S(2)}) collective-permute-start(bf16[896,256]{1,0:T(8,128)(2,1)} %refs_0_.3), channel_id=1, source_target_pairs={{0,2},{2,0},{1,3},{3,1},{4,6},{6,4},{5,7},{7,5},{8,10},{10,8},{9,1... | collective-permute-start | bytes 1376264 | tf_op jit(solution)/shard_map/ppermute | solution.py:26
  2.6 3.2 %collective-permute-start = (bf16[896,256]{1,0:T(8,128)(2,1)}, bf16[896,256]{1,0:T(8,128)(2,1)}, u32[]{:S(2)}, u32[]{:S(2)}) collective-permute-start(bf16[896,256]{1,0:T(8,128)(2,1)} %refs_0_.3), channel_id=1, source_target_pairs={{0,12},{4,0},{8,4},{12,8},{1,13},{5,1},{9,5},{13,9},{2,14},{6,2},{... | collective-permute-start | bytes 1376264 | tf_op jit(solution)/shard_map/ppermute | solution.py:26
  5.8 2.4 %convolution_convert_fusion = bf16[512,768]{1,0:T(8,128)(2,1)S(1)} fusion(bf16[896,512]{1,0:T(8,128)(2,1)S(1)} %copy-done, bf16[768,896]{1,0:T(8,128)(2,1)} %h_ref.2), kind=kOutput, calls=%fused_computation | convolution fusion | flops 705036288 | bytes 3080192 | tf_op jit(solution)/shard_map/dot_general | solution.py:293
  8.2 0.9 copy.15
  9.1 3.5 %all-to-all-start = ((bf16[4,4,32,768]{3,2,1,0:T(8,128)(2,1)}), bf16[4,4,32,768]{3,2,1,0:T(8,128)(2,1)S(1)}, u32[]{:S(2)}, u32[]{:S(2)}) async-start(bf16[4,4,32,768]{3,2,1,0:T(8,128)(2,1)} %bitcast.34), calls=%async_computation | async-start | bytes 1572864 | tf_op jit(solution)/shard_map/all_to_all | solution.py:30
  12.7 0.5 collective-permute-done.3.refs_2_
  13.2 1.4 collective-permute-done.1.refs_4_.refs_8_
  14.8 1.5 collective-permute-start.9
  16.4 1.7 %collective-permute-start.6 = (bf16[896,256]{1,0:T(8,128)(2,1)S(1)}, bf16[896,256]{1,0:T(8,128)(2,1)}, u32[]{:S(2)}, u32[]{:S(2)}) collective-permute-start(bf16[896,256]{1,0:T(8,128)(2,1)S(1)} %collective-permute-done.3.refs_2_), channel_id=1, source_target_pairs={{0,12},{4,0},{8,4},{12,8},{1,13},{5,1},{9,5},{13,9},{2,14},{6,2},{... | collective-permute-start | bytes 1376264 | tf_op jit(solution)/shard_map/ppermute | solution.py:26
  18.1 5.5 %all-to-all-done.parts = bf16[4,4,32,768]{3,2,1,0:T(8,128)(2,1)S(1)} async-done(((bf16[4,4,32,768]{3,2,1,0:T(8,128)(2,1)}), bf16[4,4,32,768]{3,2,1,0:T(8,128)(2,1)S(1)}, u32[]{:S(2)}, u32[]{:S(2)}) %all-to-all-start) | async-done | bytes 786464 | tf_op jit(solution)/shard_map/all_to_all | solution.py:30
  23.6 8.1 %partials.3 = (bf16[768,256]{1,0:T(8,128)(2,1)}, bf16[768,256]{1,0:T(8,128)(2,1)}, bf16[768,256]{1,0:T(8,128)(2,1)}, bf16[768,256]{1,0:T(8,128)(2,1)}) custom-call(s32[4]{0:T(128)S(1)} %pad_add_fusion.1.slot_of, bf16[768,896]{1,0:T(8,128)(2,1)} %h_ref.2, bf16[896,256]{1,0:T(8,128)(2,1)S(1)} %copy-done.5, ...), custom_call_target="tpu_custom_call" | custom-call | flops 8589934592 | bytes 33554432 | tf_op jit(solution)/shard_map/partials/pallas_call | solution.py:86
  31.8 1.7 %collective-permute-start.11 = (bf16[896,256]{1,0:T(8,128)(2,1)}, bf16[896,256]{1,0:T(8,128)(2,1)S(1)}, u32[]{:S(2)}, u32[]{:S(2)}) collective-permute-start(bf16[896,256]{1,0:T(8,128)(2,1)} %collective-permute-done.refs_0_.refs_4_), channel_id=1, source_target_pairs={{0,12},{4,0},{8,4},{12,8},{1,13},{5,1},{9,5},{13,9},{2,14},{6,2},{... | collective-permute-start | bytes 1376264 | tf_op jit(solution)/shard_map/ppermute | solution.py:26
  33.5 0.4 collective-permute-start.16
  33.9 1.8 %collective-permute-start.14 = (bf16[768,256]{1,0:T(8,128)(2,1)}, bf16[768,256]{1,0:T(8,128)(2,1)S(1)}, u32[]{:S(2)}, u32[]{:S(2)}) collective-permute-start(bf16[768,256]{1,0:T(8,128)(2,1)} %get-tuple-element.52), channel_id=1, source_target_pairs={{0,32},{16,48},{32,0},{48,16},{1,33},{17,49},{33,1},{49,17},{2,34}... | collective-permute-start | bytes 1179656 | tf_op jit(solution)/shard_map/ppermute | solution.py:26
  35.7 13.7 %collective-permute-done.12.refs_1_ = bf16[768,256]{1,0:T(8,128)(2,1)S(1)} collective-permute-done((bf16[768,256]{1,0:T(8,128)(2,1)}, bf16[768,256]{1,0:T(8,128)(2,1)S(1)}, u32[]{:S(2)}, u32[]{:S(2)}) %collective-permute-start.12) | collective-permute-done | bytes 393248 | tf_op jit(solution)/shard_map/ppermute | solution.py:26
  49.5 7.9 %collective-permute-done.13.refs_2_ = bf16[768,256]{1,0:T(8,128)(2,1)S(1)} collective-permute-done((bf16[768,256]{1,0:T(8,128)(2,1)}, bf16[768,256]{1,0:T(8,128)(2,1)S(1)}, u32[]{:S(2)}, u32[]{:S(2)}) %collective-permute-start.13) | collective-permute-done | bytes 393248 | tf_op jit(solution)/shard_map/ppermute | solution.py:26
  57.4 0.5 collective-permute-start.7
  58.2 0.8 copy-done.12
  58.9 0.3 collective-permute-start.17
  59.2 0.8 low_sum.1
  60.0 6.8 %all-to-all-start.1 = ((bf16[4,32,768]{2,1,0:T(8,128)(2,1)}), bf16[4,32,768]{2,1,0:T(8,128)(2,1)S(1)}, u32[]{:S(2)}, u32[]{:S(2)}) async-start(bf16[4,32,768]{2,1,0:T(8,128)(2,1)} %low_sum.1), calls=%async_computation.1 | async-start | bytes 393216 | tf_op jit(solution)/shard_map/all_to_all | solution.py:30
  66.8 0.8 copy-done.13
  67.6 7.8 %partials.4 = (bf16[384,768]{1,0:T(8,128)(2,1)}, bf16[384,768]{1,0:T(8,128)(2,1)}, bf16[384,768]{1,0:T(8,128)(2,1)}, bf16[384,768]{1,0:T(8,128)(2,1)}) custom-call(s32[4]{0:T(128)S(1)} %pad_add_fusion.1.slot_of, bf16[768,896]{1,0:T(8,128)(2,1)} %h_ref.2, bf16[896,256]{1,0:T(8,128)(2,1)} %collective-permute-done.refs_0_.refs_4_, ...), custom_call_target="tpu_custom_call" | custom-call | flops 8589934592 | bytes 33554432 | tf_op jit(solution)/shard_map/partials/pallas_call | solution.py:86
  75.4 0.3 collective-permute-start.18
  75.8 3.9 %collective-permute-start.20 = (bf16[384,768]{1,0:T(8,128)(2,1)}, bf16[384,768]{1,0:T(8,128)(2,1)}, u32[]{:S(2)}, u32[]{:S(2)}) collective-permute-start(bf16[384,768]{1,0:T(8,128)(2,1)} %get-tuple-element.62), channel_id=1, source_target_pairs={{0,32},{16,48},{32,0},{48,16},{1,33},{17,49},{33,1},{49,17},{2,34}... | collective-permute-start | bytes 1769480 | tf_op jit(solution)/shard_map/ppermute | solution.py:26
  79.6 7.8 %partials.5 = (bf16[384,768]{1,0:T(8,128)(2,1)}, bf16[384,768]{1,0:T(8,128)(2,1)}, bf16[384,768]{1,0:T(8,128)(2,1)}, bf16[384,768]{1,0:T(8,128)(2,1)}) custom-call(s32[4]{0:T(128)S(1)} %pad_add_fusion.1.slot_of, bf16[768,896]{1,0:T(8,128)(2,1)} %h_ref.2, bf16[896,256]{1,0:T(8,128)(2,1)} %collective-permute-done.refs_0_.refs_4_, ...), custom_call_target="tpu_custom_call" | custom-call | flops 8589934592 | bytes 33554432 | tf_op jit(solution)/shard_map/partials/pallas_call | solution.py:86
  87.5 5.1 %grad_partial.1 = f32[16,32,256]{2,1,0:T(8,128)} custom-call(bf16[4,32,768]{2,1,0:T(8,128)(2,1)S(1)} %all-to-all-done.1.low_ref, bf16[768,4096]{1,0:T(8,128)(2,1)} %cot_ref.2), custom_call_target="tpu_custom_call" | custom-call | flops 8589934592 | bytes 33554432 | tf_op jit(solution)/shard_map/grad_partial/pallas_call | solution.py:209
  92.6 5.7 %all-to-all-start.2 = ((f32[16,32,256]{2,1,0:T(8,128)}), f32[16,32,256]{2,1,0:T(8,128)S(1)}, u32[]{:S(2)}, u32[]{:S(2)}) async-start(f32[16,32,256]{2,1,0:T(8,128)} %grad_partial.1), calls=%async_computation.2 | async-start | bytes 1048576 | tf_op jit(solution)/shard_map/all_to_all | solution.py:30
  98.4 7.3 %collective-permute-done.20.refs_7_ = bf16[384,768]{1,0:T(8,128)(2,1)} collective-permute-done((bf16[384,768]{1,0:T(8,128)(2,1)}, bf16[384,768]{1,0:T(8,128)(2,1)}, u32[]{:S(2)}, u32[]{:S(2)}) %collective-permute-start.20) | collective-permute-done | bytes 589856 | tf_op jit(solution)/shard_map/ppermute | solution.py:26
  105.8 3.2 %collective-permute-start.25 = (bf16[384,768]{1,0:T(8,128)(2,1)S(1)}, bf16[384,768]{1,0:T(8,128)(2,1)}, u32[]{:S(2)}, u32[]{:S(2)}) collective-permute-start(bf16[384,768]{1,0:T(8,128)(2,1)S(1)} %copy-done.9), channel_id=1, source_target_pairs={{0,48},{16,0},{32,16},{48,32},{1,49},{17,1},{33,17},{49,33},{2,50}... | collective-permute-start | bytes 1769480 | tf_op jit(solution)/shard_map/ppermute | solution.py:26
  109.0 0.7 collective-permute-start.26
  109.7 3.6 %regroup.2 = (bf16[384,256]{1,0:T(8,128)(2,1)}, bf16[384,256]{1,0:T(8,128)(2,1)}, bf16[384,256]{1,0:T(8,128)(2,1)}, bf16[384,256]{1,0:T(8,128)(2,1)}) custom-call(s32[4]{0:T(128)S(1)} %pad_add_fusion.place, bf16[768,256]{1,0:T(8,128)(2,1)} %get-tuple-element.54.refs_0_, bf16[768,256]{1,0:T(8,128)(2,1)} %copy-done.14, bf16[768,256]{1,0:T(8,128)(2,1)} %copy-done.16, ...), custom_call_target="tpu_custom_call" | custom-call | flops 8589934592 | bytes 33554432 | tf_op jit(solution)/shard_map/regroup/pallas_call | solution.py:126
  113.3 2.7 %collective-permute-start.21 = (bf16[384,256]{1,0:T(8,128)(2,1)}, bf16[384,256]{1,0:T(8,128)(2,1)S(1)}, u32[]{:S(2)}, u32[]{:S(2)}) collective-permute-start(bf16[384,256]{1,0:T(8,128)(2,1)} %get-tuple-element.72), channel_id=1, source_target_pairs={{0,64},{64,128},{128,192},{192,0},{1,65},{65,129},{129,193},{193,1... | collective-permute-start | bytes 589832 | tf_op jit(solution)/shard_map/ppermute | solution.py:26
  116.0 1.5 collective-permute-start.22
  117.5 0.8 moments.1
  118.3 9.3 %all-to-all-start.3 = ((bf16[16,32,256]{2,1,0:T(8,128)(2,1)}), bf16[16,32,256]{2,1,0:T(8,128)(2,1)S(1)}, u32[]{:S(2)}, u32[]{:S(2)}) async-start(bf16[16,32,256]{2,1,0:T(8,128)(2,1)} %get-tuple-element.89), calls=%async_computation.3 | async-start | bytes 524288 | tf_op jit(solution)/shard_map/all_to_all | solution.py:30
  127.6 5.9 %collective-permute-start.23 = (bf16[384,256]{1,0:T(8,128)(2,1)}, bf16[384,256]{1,0:T(8,128)(2,1)S(1)}, u32[]{:S(2)}, u32[]{:S(2)}) collective-permute-start(bf16[384,256]{1,0:T(8,128)(2,1)} %get-tuple-element.74), channel_id=1, source_target_pairs={{0,128},{64,192},{128,0},{192,64},{1,129},{65,193},{129,1},{193,65... | collective-permute-start | bytes 589832 | tf_op jit(solution)/shard_map/ppermute | solution.py:26
  133.5 1.8 %collective-permute-done.25.refs_6_ = bf16[384,768]{1,0:T(8,128)(2,1)} collective-permute-done((bf16[384,768]{1,0:T(8,128)(2,1)S(1)}, bf16[384,768]{1,0:T(8,128)(2,1)}, u32[]{:S(2)}, u32[]{:S(2)}) %collective-permute-start.25) | collective-permute-done | bytes 589856 | tf_op jit(solution)/shard_map/ppermute | solution.py:26
  135.3 2.1 %collective-permute-done.26.refs_7_ = bf16[384,768]{1,0:T(8,128)(2,1)} collective-permute-done((bf16[384,768]{1,0:T(8,128)(2,1)S(1)}, bf16[384,768]{1,0:T(8,128)(2,1)}, u32[]{:S(2)}, u32[]{:S(2)}) %collective-permute-start.26) | collective-permute-done | bytes 589856 | tf_op jit(solution)/shard_map/ppermute | solution.py:26
  137.4 3.7 %regroup.3 = (bf16[384,256]{1,0:T(8,128)(2,1)}, bf16[384,256]{1,0:T(8,128)(2,1)}, bf16[384,256]{1,0:T(8,128)(2,1)}, bf16[384,256]{1,0:T(8,128)(2,1)}) custom-call(s32[4]{0:T(128)S(1)} %pad_add_fusion.place, bf16[768,256]{1,0:T(8,128)(2,1)} %get-tuple-element.54.refs_0_, bf16[768,256]{1,0:T(8,128)(2,1)} %copy-done.14, bf16[768,256]{1,0:T(8,128)(2,1)} %copy-done.16, ...), custom_call_target="tpu_custom_call" | custom-call | flops 8589934592 | bytes 33554432 | tf_op jit(solution)/shard_map/regroup/pallas_call | solution.py:126
  141.1 3.3 %collective-permute-start.27 = (bf16[384,256]{1,0:T(8,128)(2,1)}, bf16[384,256]{1,0:T(8,128)(2,1)S(1)}, u32[]{:S(2)}, u32[]{:S(2)}) collective-permute-start(bf16[384,256]{1,0:T(8,128)(2,1)} %get-tuple-element.81), channel_id=1, source_target_pairs={{0,64},{64,128},{128,192},{192,0},{1,65},{65,129},{129,193},{193,1... | collective-permute-start | bytes 589832 | tf_op jit(solution)/shard_map/ppermute | solution.py:26
  144.4 1.6 collective-permute-start.28
  146.0 5.8 %collective-permute-start.29 = (bf16[384,256]{1,0:T(8,128)(2,1)}, bf16[384,256]{1,0:T(8,128)(2,1)S(1)}, u32[]{:S(2)}, u32[]{:S(2)}) collective-permute-start(bf16[384,256]{1,0:T(8,128)(2,1)} %get-tuple-element.83), channel_id=1, source_target_pairs={{0,128},{64,192},{128,0},{192,64},{1,129},{65,193},{129,1},{193,65... | collective-permute-start | bytes 589832 | tf_op jit(solution)/shard_map/ppermute | solution.py:26
  151.9 13.3 %act_grad.1 = bf16[768,896]{1,0:T(8,128)(2,1)} custom-call(s32[16]{0:T(128)S(1)} %stack.107.order, bf16[768,4096]{1,0:T(8,128)(2,1)} %cot_ref.2, bf16[896,256]{1,0:T(8,128)(2,1)} %refs_0_.3, bf16[896,256]{1,0:T(8,128)(2,1)} %copy-done.7, bf16[896,256]{1,0:T(8,128)(2,1)} %copy-done.6, bf16[896,256]{1,0:T(8,128)(2,1)} %collective-permute-done.4.refs_3_, ...), custom_call_target="tpu_custom_call" | custom-call | flops 8589934592 | bytes 33554432 | tf_op jit(solution)/shard_map/act_grad/pallas_call | solution.py:272
  165.2 1.5 collective-permute-done.29.refs_7_
  166.7 0.9 finish.1
  167.6 0.5 fusion
  168.1 1.0 copy.13
  (71 shorter events, 1.1 us)
Async XLA Ops:
  0.6 5.2 %copy-start = (bf16[896,512]{1,0:T(8,128)(2,1)S(1)}, bf16[896,512]{1,0:T(8,128)(2,1)}, u32[]{:S(2)}) copy-start(bf16[896,512]{1,0:T(8,128)(2,1)} %param.9) | copy-start | bytes 2752516
  0.6 12.6 %collective-permute-start.3 = (bf16[896,256]{1,0:T(8,128)(2,1)}, bf16[896,256]{1,0:T(8,128)(2,1)S(1)}, u32[]{:S(2)}, u32[]{:S(2)}) collective-permute-start(bf16[896,256]{1,0:T(8,128)(2,1)} %refs_0_.3), channel_id=1, source_target_pairs={{0,2},{2,0},{1,3},{3,1},{4,6},{6,4},{5,7},{7,5},{8,10},{10,8},{9,1... | collective-permute-start | bytes 1376264 | tf_op jit(solution)/shard_map/ppermute | solution.py:26
  2.6 12.0 %collective-permute-start.1 = (bf16[896,256]{1,0:T(8,128)(2,1)}, bf16[896,256]{1,0:T(8,128)(2,1)S(1)}, u32[]{:S(2)}, u32[]{:S(2)}) collective-permute-start(bf16[896,256]{1,0:T(8,128)(2,1)} %refs_0_.3), channel_id=1, source_target_pairs={{0,4},{4,8},{8,12},{12,0},{1,5},{5,9},{9,13},{13,1},{2,6},{6,10},{... | collective-permute-start | bytes 1376264 | tf_op jit(solution)/shard_map/ppermute | solution.py:26
  2.6 12.1 %collective-permute-start = (bf16[896,256]{1,0:T(8,128)(2,1)}, bf16[896,256]{1,0:T(8,128)(2,1)}, u32[]{:S(2)}, u32[]{:S(2)}) collective-permute-start(bf16[896,256]{1,0:T(8,128)(2,1)} %refs_0_.3), channel_id=1, source_target_pairs={{0,12},{4,0},{8,4},{12,8},{1,13},{5,1},{9,5},{13,9},{2,14},{6,2},{... | collective-permute-start | bytes 1376264 | tf_op jit(solution)/shard_map/ppermute | solution.py:26
  8.2 4.5 %copy-start.5 = (bf16[896,256]{1,0:T(8,128)(2,1)S(1)}, bf16[896,256]{1,0:T(8,128)(2,1)}, u32[]{:S(2)}) copy-start(bf16[896,256]{1,0:T(8,128)(2,1)} %refs_0_.3) | copy-start | bytes 1376260
  9.1 14.4 %all-to-all-start = ((bf16[4,4,32,768]{3,2,1,0:T(8,128)(2,1)}), bf16[4,4,32,768]{3,2,1,0:T(8,128)(2,1)S(1)}, u32[]{:S(2)}, u32[]{:S(2)}) async-start(bf16[4,4,32,768]{3,2,1,0:T(8,128)(2,1)} %bitcast.34), calls=%async_computation | async-start | bytes 1572864 | tf_op jit(solution)/shard_map/all_to_all | solution.py:30
  12.6 10.9 %collective-permute-start.2 = (bf16[896,256]{1,0:T(8,128)(2,1)S(1)}, bf16[896,256]{1,0:T(8,128)(2,1)S(1)}, u32[]{:S(2)}, u32[]{:S(2)}) collective-permute-start(bf16[896,256]{1,0:T(8,128)(2,1)S(1)} %copy-done.5), channel_id=1, source_target_pairs={{0,1},{1,0},{2,3},{3,2},{4,5},{5,4},{6,7},{7,6},{8,9},{9,8},{10,11... | collective-permute-start | bytes 1376264 | tf_op jit(solution)/shard_map/ppermute | solution.py:26
  13.2 18.5 %copy-start.6 = (bf16[896,256]{1,0:T(8,128)(2,1)}, bf16[896,256]{1,0:T(8,128)(2,1)S(1)}, u32[]{:S(2)}) copy-start(bf16[896,256]{1,0:T(8,128)(2,1)S(1)} %collective-permute-done.3.refs_2_) | copy-start | bytes 1376260
  14.6 19.3 %copy-start.10 = (bf16[896,256]{1,0:T(8,128)(2,1)}, bf16[896,256]{1,0:T(8,128)(2,1)S(1)}, u32[]{:S(2)}) copy-start(bf16[896,256]{1,0:T(8,128)(2,1)S(1)} %collective-permute-done.1.refs_4_.refs_8_) | copy-start | bytes 1376260
  14.7 8.9 %collective-permute-start.4 = (bf16[896,256]{1,0:T(8,128)(2,1)S(1)}, bf16[896,256]{1,0:T(8,128)(2,1)}, u32[]{:S(2)}, u32[]{:S(2)}) collective-permute-start(bf16[896,256]{1,0:T(8,128)(2,1)S(1)} %collective-permute-done.3.refs_2_), channel_id=1, source_target_pairs={{0,1},{1,0},{2,3},{3,2},{4,5},{5,4},{6,7},{7,6},{8,9},{9,8},{10,11... | collective-permute-start | bytes 1376264 | tf_op jit(solution)/shard_map/ppermute | solution.py:26
  14.8 18.7 %collective-permute-start.9 = (bf16[896,256]{1,0:T(8,128)(2,1)S(1)}, bf16[896,256]{1,0:T(8,128)(2,1)}, u32[]{:S(2)}, u32[]{:S(2)}) collective-permute-start(bf16[896,256]{1,0:T(8,128)(2,1)S(1)} %collective-permute-done.3.refs_2_), channel_id=1, source_target_pairs={{0,4},{4,8},{8,12},{12,0},{1,5},{5,9},{9,13},{13,1},{2,6},{6,10},{... | collective-permute-start | bytes 1376264 | tf_op jit(solution)/shard_map/ppermute | solution.py:26
  16.4 15.4 %collective-permute-start.6 = (bf16[896,256]{1,0:T(8,128)(2,1)S(1)}, bf16[896,256]{1,0:T(8,128)(2,1)}, u32[]{:S(2)}, u32[]{:S(2)}) collective-permute-start(bf16[896,256]{1,0:T(8,128)(2,1)S(1)} %collective-permute-done.3.refs_2_), channel_id=1, source_target_pairs={{0,12},{4,0},{8,4},{12,8},{1,13},{5,1},{9,5},{13,9},{2,14},{6,2},{... | collective-permute-start | bytes 1376264 | tf_op jit(solution)/shard_map/ppermute | solution.py:26
  23.6 8.1 %copy-start.7 = (bf16[896,256]{1,0:T(8,128)(2,1)}, bf16[896,256]{1,0:T(8,128)(2,1)S(1)}, u32[]{:S(2)}) copy-start(bf16[896,256]{1,0:T(8,128)(2,1)S(1)} %collective-permute-done.2.refs_1_) | copy-start | bytes 1376260
  31.7 17.7 %collective-permute-start.12 = (bf16[768,256]{1,0:T(8,128)(2,1)}, bf16[768,256]{1,0:T(8,128)(2,1)S(1)}, u32[]{:S(2)}, u32[]{:S(2)}) collective-permute-start(bf16[768,256]{1,0:T(8,128)(2,1)} %get-tuple-element.51), channel_id=1, source_target_pairs={{0,16},{16,32},{32,48},{48,0},{1,17},{17,33},{33,49},{49,1},{2,18}... | collective-permute-start | bytes 1179656 | tf_op jit(solution)/shard_map/ppermute | solution.py:26
  31.8 25.6 %collective-permute-start.11 = (bf16[896,256]{1,0:T(8,128)(2,1)}, bf16[896,256]{1,0:T(8,128)(2,1)S(1)}, u32[]{:S(2)}, u32[]{:S(2)}) collective-permute-start(bf16[896,256]{1,0:T(8,128)(2,1)} %collective-permute-done.refs_0_.refs_4_), channel_id=1, source_target_pairs={{0,12},{4,0},{8,4},{12,8},{1,13},{5,1},{9,5},{13,9},{2,14},{6,2},{... | collective-permute-start | bytes 1376264 | tf_op jit(solution)/shard_map/ppermute | solution.py:26
  33.5 24.4 %collective-permute-start.16 = (bf16[896,256]{1,0:T(8,128)(2,1)}, bf16[896,256]{1,0:T(8,128)(2,1)}, u32[]{:S(2)}, u32[]{:S(2)}) collective-permute-start(bf16[896,256]{1,0:T(8,128)(2,1)} %collective-permute-done.9.refs_6_.refs_10_), channel_id=1, source_target_pairs={{0,4},{4,8},{8,12},{12,0},{1,5},{5,9},{9,13},{13,1},{2,6},{6,10},{... | collective-permute-start | bytes 1376264 | tf_op jit(solution)/shard_map/ppermute | solution.py:26
  33.9 24.1 %collective-permute-start.8 = (bf16[896,256]{1,0:T(8,128)(2,1)S(1)}, bf16[896,256]{1,0:T(8,128)(2,1)S(1)}, u32[]{:S(2)}, u32[]{:S(2)}) collective-permute-start(bf16[896,256]{1,0:T(8,128)(2,1)S(1)} %collective-permute-done.1.refs_4_.refs_8_), channel_id=1, source_target_pairs={{0,1},{1,0},{2,3},{3,2},{4,5},{5,4},{6,7},{7,6},{8,9},{9,8},{10,11... | collective-permute-start | bytes 1376264 | tf_op jit(solution)/shard_map/ppermute | solution.py:26
  33.9 15.5 %collective-permute-start.14 = (bf16[768,256]{1,0:T(8,128)(2,1)}, bf16[768,256]{1,0:T(8,128)(2,1)S(1)}, u32[]{:S(2)}, u32[]{:S(2)}) collective-permute-start(bf16[768,256]{1,0:T(8,128)(2,1)} %get-tuple-element.52), channel_id=1, source_target_pairs={{0,32},{16,48},{32,0},{48,16},{1,33},{17,49},{33,1},{49,17},{2,34}... | collective-permute-start | bytes 1179656 | tf_op jit(solution)/shard_map/ppermute | solution.py:26
  49.4 8.6 %copy-start.14 = (bf16[768,256]{1,0:T(8,128)(2,1)}, bf16[768,256]{1,0:T(8,128)(2,1)S(1)}, u32[]{:S(2)}) copy-start(bf16[768,256]{1,0:T(8,128)(2,1)S(1)} %collective-permute-done.12.refs_1_) | copy-start | bytes 1179652
  49.4 8.0 %collective-permute-start.13 = (bf16[768,256]{1,0:T(8,128)(2,1)}, bf16[768,256]{1,0:T(8,128)(2,1)S(1)}, u32[]{:S(2)}, u32[]{:S(2)}) collective-permute-start(bf16[768,256]{1,0:T(8,128)(2,1)} %get-tuple-element.53), channel_id=1, source_target_pairs={{0,48},{16,0},{32,16},{48,32},{1,49},{17,1},{33,17},{49,33},{2,50}... | collective-permute-start | bytes 1179656 | tf_op jit(solution)/shard_map/ppermute | solution.py:26
  49.4 8.6 %copy-start.15 = (bf16[768,256]{1,0:T(8,128)(2,1)}, bf16[768,256]{1,0:T(8,128)(2,1)S(1)}, u32[]{:S(2)}) copy-start(bf16[768,256]{1,0:T(8,128)(2,1)S(1)} %collective-permute-done.14.refs_3_) | copy-start | bytes 1179652
  49.4 17.4 %collective-permute-start.5 = (bf16[896,256]{1,0:T(8,128)(2,1)}, bf16[896,256]{1,0:T(8,128)(2,1)}, u32[]{:S(2)}, u32[]{:S(2)}) collective-permute-start(bf16[896,256]{1,0:T(8,128)(2,1)} %collective-permute-done.refs_0_.refs_4_), channel_id=1, source_target_pairs={{0,1},{1,0},{2,3},{3,2},{4,5},{5,4},{6,7},{7,6},{8,9},{9,8},{10,11... | collective-permute-start | bytes 1376264 | tf_op jit(solution)/shard_map/ppermute | solution.py:26
  57.4 9.4 %collective-permute-start.10 = (bf16[896,256]{1,0:T(8,128)(2,1)}, bf16[896,256]{1,0:T(8,128)(2,1)}, u32[]{:S(2)}, u32[]{:S(2)}) collective-permute-start(bf16[896,256]{1,0:T(8,128)(2,1)} %collective-permute-done.9.refs_6_.refs_10_), channel_id=1, source_target_pairs={{0,1},{1,0},{2,3},{3,2},{4,5},{5,4},{6,7},{7,6},{8,9},{9,8},{10,11... | collective-permute-start | bytes 1376264 | tf_op jit(solution)/shard_map/ppermute | solution.py:26
  57.4 2.6 %copy-start.11 = (bf16[896,256]{1,0:T(8,128)(2,1)}, bf16[896,256]{1,0:T(8,128)(2,1)S(1)}, u32[]{:S(2)}) copy-start(bf16[896,256]{1,0:T(8,128)(2,1)S(1)} %collective-permute-done.11.refs_8_.refs_12_) | copy-start | bytes 1376260
  57.4 9.4 %collective-permute-start.7 = (bf16[896,256]{1,0:T(8,128)(2,1)}, bf16[896,256]{1,0:T(8,128)(2,1)}, u32[]{:S(2)}, u32[]{:S(2)}) collective-permute-start(bf16[896,256]{1,0:T(8,128)(2,1)} %collective-permute-done.6.refs_2_.refs_6_), channel_id=1, source_target_pairs={{0,1},{1,0},{2,3},{3,2},{4,5},{5,4},{6,7},{7,6},{8,9},{9,8},{10,11... | collective-permute-start | bytes 1376264 | tf_op jit(solution)/shard_map/ppermute | solution.py:26
  57.9 8.9 %collective-permute-start.15 = (bf16[896,256]{1,0:T(8,128)(2,1)S(1)}, bf16[896,256]{1,0:T(8,128)(2,1)}, u32[]{:S(2)}, u32[]{:S(2)}) collective-permute-start(bf16[896,256]{1,0:T(8,128)(2,1)S(1)} %collective-permute-done.11.refs_8_.refs_12_), channel_id=1, source_target_pairs={{0,1},{1,0},{2,3},{3,2},{4,5},{5,4},{6,7},{7,6},{8,9},{9,8},{10,11... | collective-permute-start | bytes 1376264 | tf_op jit(solution)/shard_map/ppermute | solution.py:26
  58.9 7.9 %collective-permute-start.17 = (bf16[896,256]{1,0:T(8,128)(2,1)}, bf16[896,256]{1,0:T(8,128)(2,1)S(1)}, u32[]{:S(2)}, u32[]{:S(2)}) collective-permute-start(bf16[896,256]{1,0:T(8,128)(2,1)} %collective-permute-done.16.refs_10_.refs_14_), channel_id=1, source_target_pairs={{0,1},{1,0},{2,3},{3,2},{4,5},{5,4},{6,7},{7,6},{8,9},{9,8},{10,11... | collective-permute-start | bytes 1376264 | tf_op jit(solution)/shard_map/ppermute | solution.py:26
  60.0 27.5 %all-to-all-start.1 = ((bf16[4,32,768]{2,1,0:T(8,128)(2,1)}), bf16[4,32,768]{2,1,0:T(8,128)(2,1)S(1)}, u32[]{:S(2)}, u32[]{:S(2)}) async-start(bf16[4,32,768]{2,1,0:T(8,128)(2,1)} %low_sum.1), calls=%async_computation.1 | async-start | bytes 393216 | tf_op jit(solution)/shard_map/all_to_all | solution.py:30
  75.4 23.0 %collective-permute-start.18 = (bf16[384,768]{1,0:T(8,128)(2,1)}, bf16[384,768]{1,0:T(8,128)(2,1)}, u32[]{:S(2)}, u32[]{:S(2)}) collective-permute-start(bf16[384,768]{1,0:T(8,128)(2,1)} %get-tuple-element.61), channel_id=1, source_target_pairs={{0,16},{16,32},{32,48},{48,0},{1,17},{17,33},{33,49},{49,1},{2,18}... | collective-permute-start | bytes 1769480 | tf_op jit(solution)/shard_map/ppermute | solution.py:26
  75.8 30.0 %collective-permute-start.20 = (bf16[384,768]{1,0:T(8,128)(2,1)}, bf16[384,768]{1,0:T(8,128)(2,1)}, u32[]{:S(2)}, u32[]{:S(2)}) collective-permute-start(bf16[384,768]{1,0:T(8,128)(2,1)} %get-tuple-element.62), channel_id=1, source_target_pairs={{0,32},{16,48},{32,0},{48,16},{1,33},{17,49},{33,1},{49,17},{2,34}... | collective-permute-start | bytes 1769480 | tf_op jit(solution)/shard_map/ppermute | solution.py:26
  79.6 26.1 %collective-permute-start.19 = (bf16[384,768]{1,0:T(8,128)(2,1)}, bf16[384,768]{1,0:T(8,128)(2,1)}, u32[]{:S(2)}, u32[]{:S(2)}) collective-permute-start(bf16[384,768]{1,0:T(8,128)(2,1)} %get-tuple-element.63), channel_id=1, source_target_pairs={{0,48},{16,0},{32,16},{48,32},{1,49},{17,1},{33,17},{49,33},{2,50}... | collective-permute-start | bytes 1769480 | tf_op jit(solution)/shard_map/ppermute | solution.py:26
  87.4 18.3 %copy-start.9 = (bf16[384,768]{1,0:T(8,128)(2,1)S(1)}, bf16[384,768]{1,0:T(8,128)(2,1)}, u32[]{:S(2)}) copy-start(bf16[384,768]{1,0:T(8,128)(2,1)} %get-tuple-element.78) | copy-start | bytes 1769476
  87.5 21.5 %copy-start.8 = (bf16[384,768]{1,0:T(8,128)(2,1)S(1)}, bf16[384,768]{1,0:T(8,128)(2,1)}, u32[]{:S(2)}) copy-start(bf16[384,768]{1,0:T(8,128)(2,1)} %get-tuple-element.79) | copy-start | bytes 1769476
  92.6 24.9 %all-to-all-start.2 = ((f32[16,32,256]{2,1,0:T(8,128)}), f32[16,32,256]{2,1,0:T(8,128)S(1)}, u32[]{:S(2)}, u32[]{:S(2)}) async-start(f32[16,32,256]{2,1,0:T(8,128)} %grad_partial.1), calls=%async_computation.2 | async-start | bytes 1048576 | tf_op jit(solution)/shard_map/all_to_all | solution.py:30
  98.4 19.1 %copy-start.3 = (f32[32,256]{1,0:T(8,128)S(1)}, f32[32,256]{1,0:T(8,128)}, u32[]{:S(2)}) copy-start(f32[32,256]{1,0:T(8,128)} %first.1) | copy-start | bytes 98308
  98.4 19.1 %copy-start.4 = (f32[32,256]{1,0:T(8,128)S(1)}, f32[32,256]{1,0:T(8,128)}, u32[]{:S(2)}) copy-start(f32[32,256]{1,0:T(8,128)} %second.1) | copy-start | bytes 98308
  105.7 21.8 %collective-permute-start.24 = (bf16[384,768]{1,0:T(8,128)(2,1)}, bf16[384,768]{1,0:T(8,128)(2,1)}, u32[]{:S(2)}, u32[]{:S(2)}) collective-permute-start(bf16[384,768]{1,0:T(8,128)(2,1)} %get-tuple-element.77), channel_id=1, source_target_pairs={{0,16},{16,32},{32,48},{48,0},{1,17},{17,33},{33,49},{49,1},{2,18}... | collective-permute-start | bytes 1769480 | tf_op jit(solution)/shard_map/ppermute | solution.py:26
  105.8 29.6 %collective-permute-start.25 = (bf16[384,768]{1,0:T(8,128)(2,1)S(1)}, bf16[384,768]{1,0:T(8,128)(2,1)}, u32[]{:S(2)}, u32[]{:S(2)}) collective-permute-start(bf16[384,768]{1,0:T(8,128)(2,1)S(1)} %copy-done.9), channel_id=1, source_target_pairs={{0,48},{16,0},{32,16},{48,32},{1,49},{17,1},{33,17},{49,33},{2,50}... | collective-permute-start | bytes 1769480 | tf_op jit(solution)/shard_map/ppermute | solution.py:26
  109.0 28.5 %collective-permute-start.26 = (bf16[384,768]{1,0:T(8,128)(2,1)S(1)}, bf16[384,768]{1,0:T(8,128)(2,1)}, u32[]{:S(2)}, u32[]{:S(2)}) collective-permute-start(bf16[384,768]{1,0:T(8,128)(2,1)S(1)} %copy-done.8), channel_id=1, source_target_pairs={{0,32},{16,48},{32,0},{48,16},{1,33},{17,49},{33,1},{49,17},{2,34}... | collective-permute-start | bytes 1769480 | tf_op jit(solution)/shard_map/ppermute | solution.py:26
  113.3 32.7 %collective-permute-start.21 = (bf16[384,256]{1,0:T(8,128)(2,1)}, bf16[384,256]{1,0:T(8,128)(2,1)S(1)}, u32[]{:S(2)}, u32[]{:S(2)}) collective-permute-start(bf16[384,256]{1,0:T(8,128)(2,1)} %get-tuple-element.72), channel_id=1, source_target_pairs={{0,64},{64,128},{128,192},{192,0},{1,65},{65,129},{129,193},{193,1... | collective-permute-start | bytes 589832 | tf_op jit(solution)/shard_map/ppermute | solution.py:26
  116.0 49.2 %collective-permute-start.22 = (bf16[384,256]{1,0:T(8,128)(2,1)}, bf16[384,256]{1,0:T(8,128)(2,1)S(1)}, u32[]{:S(2)}, u32[]{:S(2)}) collective-permute-start(bf16[384,256]{1,0:T(8,128)(2,1)} %get-tuple-element.73), channel_id=1, source_target_pairs={{0,192},{64,0},{128,64},{192,128},{1,193},{65,1},{129,65},{193,129... | collective-permute-start | bytes 589832 | tf_op jit(solution)/shard_map/ppermute | solution.py:26
  118.3 49.3 %all-to-all-start.3 = ((bf16[16,32,256]{2,1,0:T(8,128)(2,1)}), bf16[16,32,256]{2,1,0:T(8,128)(2,1)S(1)}, u32[]{:S(2)}, u32[]{:S(2)}) async-start(bf16[16,32,256]{2,1,0:T(8,128)(2,1)} %get-tuple-element.89), calls=%async_computation.3 | async-start | bytes 524288 | tf_op jit(solution)/shard_map/all_to_all | solution.py:30
  127.6 37.6 %collective-permute-start.23 = (bf16[384,256]{1,0:T(8,128)(2,1)}, bf16[384,256]{1,0:T(8,128)(2,1)S(1)}, u32[]{:S(2)}, u32[]{:S(2)}) collective-permute-start(bf16[384,256]{1,0:T(8,128)(2,1)} %get-tuple-element.74), channel_id=1, source_target_pairs={{0,128},{64,192},{128,0},{192,64},{1,129},{65,193},{129,1},{193,65... | collective-permute-start | bytes 589832 | tf_op jit(solution)/shard_map/ppermute | solution.py:26
  141.1 24.1 %collective-permute-start.27 = (bf16[384,256]{1,0:T(8,128)(2,1)}, bf16[384,256]{1,0:T(8,128)(2,1)S(1)}, u32[]{:S(2)}, u32[]{:S(2)}) collective-permute-start(bf16[384,256]{1,0:T(8,128)(2,1)} %get-tuple-element.81), channel_id=1, source_target_pairs={{0,64},{64,128},{128,192},{192,0},{1,65},{65,129},{129,193},{193,1... | collective-permute-start | bytes 589832 | tf_op jit(solution)/shard_map/ppermute | solution.py:26
  144.4 20.8 %collective-permute-start.28 = (bf16[384,256]{1,0:T(8,128)(2,1)}, bf16[384,256]{1,0:T(8,128)(2,1)S(1)}, u32[]{:S(2)}, u32[]{:S(2)}) collective-permute-start(bf16[384,256]{1,0:T(8,128)(2,1)} %get-tuple-element.82), channel_id=1, source_target_pairs={{0,192},{64,0},{128,64},{192,128},{1,193},{65,1},{129,65},{193,129... | collective-permute-start | bytes 589832 | tf_op jit(solution)/shard_map/ppermute | solution.py:26
  146.0 20.7 %copy-start.1 = (bf16[384,256]{1,0:T(8,128)(2,1)S(1)}, bf16[384,256]{1,0:T(8,128)(2,1)}, u32[]{:S(2)}) copy-start(bf16[384,256]{1,0:T(8,128)(2,1)} %get-tuple-element.71.refs_0_) | copy-start | bytes 589828
  146.0 20.7 %copy-start.2 = (bf16[384,256]{1,0:T(8,128)(2,1)S(1)}, bf16[384,256]{1,0:T(8,128)(2,1)}, u32[]{:S(2)}) copy-start(bf16[384,256]{1,0:T(8,128)(2,1)} %get-tuple-element.80.refs_4_) | copy-start | bytes 589828
  146.0 20.7 %collective-permute-start.29 = (bf16[384,256]{1,0:T(8,128)(2,1)}, bf16[384,256]{1,0:T(8,128)(2,1)S(1)}, u32[]{:S(2)}, u32[]{:S(2)}) collective-permute-start(bf16[384,256]{1,0:T(8,128)(2,1)} %get-tuple-element.83), channel_id=1, source_target_pairs={{0,128},{64,192},{128,0},{192,64},{1,129},{65,193},{129,1},{193,65... | collective-permute-start | bytes 589832 | tf_op jit(solution)/shard_map/ppermute | solution.py:26
  (3 other events, 2.4 us)
